TPU v7x, 32 devices: a whole 2x2x4 slice. The times are simulated.
32 devices in a mesh: gx: 4 (over z), gy: 8 (over y, x, core).
Axes of the slice: x: 2, y: 2, z: 4, core: 2. Of those that a mesh axis runs over, the one named last changes fastest.
Arguments:
- particles: float32 [384, 6, 128], P(('gx', 'gy')), may hold values from -6 to 6
- occupancy: int32 [384], P(('gx', 'gy')), may hold values from 32 to 128, as said below
- neighbours: int32 [384, 16], P(('gx', 'gy')), may hold values from 0 to 383, as said below
- curve_cuts: int32 [2, 32], replicated, may hold values from 0 to 378, as said below
Outputs:
- after_first: float32 [768, 6, 128], P(('gx', 'gy'))
- after_second: float32 [768, 6, 128], P(('gx', 'gy'))
Inputs may be any that keep to these rules, and one draw needn't show every extreme that they name: `occupancy`: each tile holds at least 32 live particles, and some tile in every draw holds 128. `neighbours`: tile t lists 16 different tiles among the curve positions t + 1 to t + 24, counted modulo 384. `curve_cuts`: entry d of each row is d * 12 + e with e between -6 and 6, and e is 0 for device 0; so each device owns 0 to 24 tiles, and in every step some device owns exactly 24.
All inputs are finite; a program needn't handle non-finite values.
Results may differ from a plain program's by a relative error of at most 0.0001.
Values sent between devices are 32-bit elements; how exact they have to be, the bound alone decides.
No kernel may reach another device: no remote copies, remote signals or barrier semaphores. Data moves between devices by JAX's collectives and lax.ppermute only.
A program may use at most 64 MiB of HBM per device.

v0:
```python
import functools

import jax
import jax.numpy as jnp
from jax import lax
from jax.experimental import pallas as pl
from jax.experimental.pallas import tpu as pltpu
from jax.sharding import PartitionSpec as P

AXES = ("gx", "gy")
STEPS = 2

soften = 0.05
time_step = 0.5
reach = 2
chunk = 4
units = 12
feature_rows = 32
far_norm = 1e36
lanes = 128
block_rows = 32
vmem_limit = 16 << 20


def swapped(value, first, wrap=True):
    count = lax.axis_size(AXES)
    pairs = []
    for lower in range(first, count, 2):
        if wrap or lower + 1 < count:
            upper = (lower + 1) % count
            pairs += [(lower, upper), (upper, lower)]
    return lax.ppermute(value, AXES, pairs)


def round_up(value, step):
    return -(-value // step) * step


def device_index():
    return lax.axis_index("gx") * lax.axis_size("gy") + lax.axis_index("gy")


def pieces(value, count):
    parts = []
    rest = value
    for _ in range(count - 1):
        part = rest.astype(jnp.bfloat16).astype(jnp.float32)
        parts.append(part)
        rest = rest - part
    parts.append(rest.astype(jnp.bfloat16).astype(jnp.float32))
    return parts


def pack_kernel(total_tiles, particles_ref, occupancy_ref, neighbours_ref, packed_ref, speed_ref):
    tiles, slots = (particles_ref.shape[0], particles_ref.shape[2])
    listed = neighbours_ref.shape[1]
    for row in range(3):
        packed_ref[row * tiles : (row + 1) * tiles, :] = particles_ref[:, row, :]
        speed_ref[row * tiles : (row + 1) * tiles, :] = particles_ref[:, 3 + row, :]
    tile_ids = lax.broadcasted_iota(jnp.int32, (tiles, listed), 0)
    offsets = neighbours_ref[...] - (device_index() * tiles + tile_ids)
    offsets = jnp.where(offsets < 0, offsets + total_tiles, offsets)
    packed_ref[3 * tiles :, :] = jnp.zeros((tiles, slots), jnp.float32)
    packed_ref[3 * tiles :, :listed] = offsets.astype(jnp.float32)
    for tile in range(tiles):
        live = occupancy_ref[tile].astype(jnp.float32)
        packed_ref[3 * tiles + tile : 3 * tiles + tile + 1, listed : listed + 1] = jnp.full((1, 1), live)


def places_of(index, tiles, offsets):
    place = index + offsets[0]
    for block in range(1, len(offsets)):
        place = jnp.where(index >= block * tiles, index - block * tiles + offsets[block], place)
    return jnp.where(index >= len(offsets) * tiles, -1000.0, place)


def build_lists(aux, own, tiles, listed, offsets):
    rows = aux.shape[0]
    dummy = len(offsets) * tiles
    index = lax.broadcasted_iota(jnp.int32, (rows, lanes), 0).astype(jnp.float32)
    lane = lax.broadcasted_iota(jnp.int32, (rows, lanes), 1).astype(jnp.float32)
    place = places_of(index, tiles, offsets)
    mask = place == lane
    for entry in range(listed):
        mask = mask | (place + aux[:, entry : entry + 1] == lane)
    own_rows = own.shape[0]
    own_index = lax.broadcasted_iota(jnp.int32, (own_rows, lanes), 0).astype(jnp.float32)
    own_lane = lax.broadcasted_iota(jnp.int32, (own_rows, lanes), 1).astype(jnp.float32)
    own_place = places_of(own_lane, tiles, offsets)
    listing = own_index + own[:, 0:1] == own_place
    for entry in range(1, listed):
        listing = listing | (own_index + own[:, entry : entry + 1] == own_place)
    listing = jnp.where(listing, 1.0, 0.0)
    listing = jnp.concatenate([listing, jnp.zeros((lanes - own_rows, lanes), jnp.float32)], axis=0)
    listing = jnp.transpose(listing)[:rows]
    mask = jnp.maximum(jnp.where(mask, 1.0, 0.0), listing)
    mask = jnp.where((lane < tiles) & (index < dummy), mask, 0.0)
    earlier = lax.broadcasted_iota(jnp.int32, (rows, rows), 1) < lax.broadcasted_iota(jnp.int32, (rows, rows), 0)
    rank = jnp.dot(
        jnp.where(earlier, 1.0, 0.0).astype(jnp.bfloat16),
        mask.astype(jnp.bfloat16),
        preferred_element_type=jnp.float32,
    )
    key = jnp.where(mask > 0.5, rank, -1.0)
    counts = jnp.sum(mask, axis=0, keepdims=True)
    lists = []
    for tile in range(tiles):
        hit = key[:, tile : tile + 1] == lane
        row = jnp.sum(jnp.where(hit, index - dummy, 0.0), axis=0, keepdims=True) + dummy
        live = own[tile : tile + 1, listed : listed + 1]
        blocks = jnp.full((1, 1), 1.0)
        for filled in range(block_rows, lanes, block_rows):
            blocks = blocks + jnp.where(live > filled, 1.0, 0.0)
        lists.append(jnp.where(lane[:1] == lanes - 1, blocks, row))
    lists.append(jnp.where(lane[:1] == lanes - 1, 1.0, float(dummy)))
    lists.append(counts)
    return [row.astype(jnp.int32) for row in lists]


def middles(own_place):
    return [jnp.mean(axis[:8], keepdims=True) for axis in own_place]


def feature_of(feature_ref, tile):
    return feature_ref[tile * feature_rows : (tile + 1) * feature_rows, :]


def build_sources(places, middle, weight, feature_ref, moment_ref, source_ref):
    rows = weight.shape[0]
    ones = jnp.ones_like(weight)
    zeros = jnp.zeros_like(weight)
    features = []
    norm = zeros
    for axis in range(3):
        value = weight * (places[axis] - middle[axis])
        norm = norm + value * value
        moment_ref.reshape(rows * 8, lanes)[pl.ds(axis, rows, 8), :] = value
        high, mid, low = pieces(value, 3)
        features += [high, high, mid, mid, high, low]
    features += pieces(jnp.where(weight > 0.5, norm, far_norm), 3) + [ones] * 3
    features += [zeros] * (feature_rows - len(features))
    for row, value in enumerate(features):
        feature_ref[pl.ds(row, rows, feature_rows), :] = value
    for tile in range(rows):
        source_ref[tile] = feature_of(feature_ref, tile).astype(jnp.bfloat16)


def build_targets(own_place, middle, feature_ref, target_ref):
    tiles = own_place[0].shape[0]
    ones = jnp.ones_like(own_place[0])
    zeros = jnp.zeros_like(own_place[0])
    features = []
    norm = zeros
    for axis in range(3):
        value = own_place[axis] - middle[axis]
        norm = norm + value * value
        high, mid, low = [-2.0 * part for part in pieces(value, 3)]
        features += [high, mid, high, mid, low, high]
    features += [ones] * 3 + pieces(norm + soften, 3)
    features += [zeros] * (feature_rows - len(features))
    for row, value in enumerate(features):
        feature_ref[pl.ds(row, tiles, feature_rows), :] = value
    blank = jnp.zeros((lanes - feature_rows, lanes), jnp.float32)
    blocks = lanes // block_rows
    for tile in range(tiles):
        turned = jnp.transpose(jnp.concatenate([feature_of(feature_ref, tile), blank], axis=0))
        turned = turned[:, :feature_rows].astype(jnp.bfloat16)
        for block in range(blocks):
            target_ref[tile * blocks + block] = turned[block * block_rows : (block + 1) * block_rows]
    target_ref[tiles * blocks] = target_ref[0]


def accumulate(tiles, lists_ref, source_ref, target_ref, moment_ref, total_ref):
    blocks = lanes // block_rows
    item_counts = [
        jnp.maximum((lists_ref[tiles + 1, tile] + chunk - 1) // chunk, 1) * lists_ref[tile, lanes - 1] for tile in range(tiles)
    ]
    item_total = functools.reduce(lambda left, right: left + right, item_counts)

    def following(tile, block, part):
        more = (part + 1) * chunk < lists_ref[tiles + 1, tile]
        again = block + 1 < lists_ref[tile, lanes - 1]
        return (
            jnp.where(more | again, tile, jnp.minimum(tile + 1, tiles)),
            jnp.where(more, block, jnp.where(again, block + 1, 0)),
            jnp.where(more, part + 1, 0),
        )

    def sources_of(tile, part):
        return [lists_ref[tile, part * chunk + entry] for entry in range(chunk)]

    def distances(spot, sources):
        target = target_ref[spot]
        features = [source_ref[source] for source in sources]
        return [
            jnp.dot(target, jnp.concatenate(features[first : first + 2], axis=1), preferred_element_type=jnp.float32)
            for first in range(0, chunk, 2)
        ]

    def kernels(spot, places, squares):
        for first in range(0, block_rows, 8):
            strip = slice(first, first + 8)
            sums = [total_ref[spot, row, strip, :] for row in range(4)]
            for entry in range(chunk):
                column = (entry % 2) * lanes
                inverse = lax.rsqrt(squares[entry // 2][strip, column : column + lanes])
                kernel = inverse * inverse * inverse
                for axis in range(3):
                    sums[axis] = sums[axis] + kernel * places[entry][axis]
                sums[3] = sums[3] + kernel
            for row in range(4):
                total_ref[spot, row, strip, :] = sums[row]

    def step(_, carry):
        tile, block, part = carry
        waiting = None
        for _ in range(units):
            sources = sources_of(tile, part)
            places = [
                [jnp.broadcast_to(moment_ref[source, axis : axis + 1, :], (8, lanes)) for axis in range(3)]
                for source in sources
            ]
            spot = tile * blocks + block
            item = (spot, places, distances(spot, sources))
            if waiting is not None:
                kernels(*waiting)
            waiting = item
            tile, block, part = following(tile, block, part)
        kernels(*waiting)
        return (tile, block, part)

    zero = jnp.int32(0)
    lax.fori_loop(0, (item_total + units - 1) // units, step, (zero, zero, zero))


def advance(middle, place_own, speed_own, weight_own, total_ref, sums_ref):
    tiles = weight_own.shape[0]
    blocks = lanes // block_rows
    for tile in range(tiles):
        for row in range(4):
            parts = [total_ref[tile * blocks + block, row] for block in range(blocks)]
            total = jnp.sum(jnp.transpose(jnp.concatenate(parts, axis=0)), axis=0, keepdims=True)
            sums_ref[row, tile : tile + 1, :] = total
    zeroth = sums_ref[3, :tiles, :]
    places, speeds = ([], [])
    for axis in range(3):
        force = sums_ref[axis, :tiles, :] - (place_own[axis] - middle[axis]) * zeroth
        speeds.append(weight_own * (speed_own[axis] + time_step * force / lanes))
        places.append(weight_own * (place_own[axis] + time_step * speeds[axis]))
    return places, speeds


def part_of(ref, tiles, row):
    return ref[row * tiles : (row + 1) * tiles, :]


def fill_planes(planes, tiles, blocks):
    kinds, rows, slots = planes.shape
    filled = len(blocks) * tiles
    planes[:, filled:, :] = jnp.zeros((kinds, rows - filled, slots), jnp.float32)
    for block, ref in enumerate(blocks):
        for kind in range(kinds):
            planes[kind, block * tiles : (block + 1) * tiles, :] = part_of(ref, tiles, kind)


def weights_of(aux, listed):
    slot = lax.broadcasted_iota(jnp.int32, aux.shape, 1).astype(jnp.float32)
    return jnp.where(slot < aux[:, listed : listed + 1], 1.0, 0.0)


def offsets_of(tiles, near_pair):
    device = device_index()
    toward = jnp.where(device % 2 == 0, 1.0, -1.0) * float(tiles)
    if near_pair:
        return [0.0, toward]
    return [-toward, -reach * toward, reach * toward]


def far_blocks(pair, forwarded, first_rows):
    return (pair[:first_rows, :], pair[first_rows:, :], forwarded[:first_rows, :])


def prepare(first, near_pair, listed, own_ref, blocks, lists_ref, weight_ref, tools):
    planes, scalars, copy_sem, feature_ref, moment_ref, source_ref = tools
    tiles = own_ref.shape[0] // planes.shape[0]
    if not first:
        copy = pltpu.make_async_copy(lists_ref, scalars, copy_sem)
        copy.start()
    fill_planes(planes, tiles, blocks)
    if first:
        aux = planes[3]
        own_aux = jnp.concatenate(
            [part_of(own_ref, tiles, 3), jnp.zeros((round_up(tiles, 8) - tiles, lanes), jnp.float32)], axis=0
        )
        for row, value in enumerate(build_lists(aux, own_aux, tiles, listed, offsets_of(tiles, near_pair))):
            lists_ref[row : row + 1, :] = value
        copy = pltpu.make_async_copy(lists_ref, scalars, copy_sem)
        copy.start()
        weight_ref[...] = weights_of(aux, listed)
    middle = middles([part_of(own_ref, tiles, axis) for axis in range(3)])
    build_sources([planes[axis] for axis in range(3)], middle, weight_ref[...], feature_ref, moment_ref, source_ref)
    return middle, copy


def begin(listed, first, *refs):
    if first:
        own_ref, sibling_ref, total_ref, target_ref, lists_ref, weight_ref, *scratch = refs
    else:
        own_ref, sibling_ref, lists_ref, weight_ref, total_ref, target_ref, *scratch = refs
    tools = scratch
    tiles = own_ref.shape[0] // tools[0].shape[0]
    middle, copy = prepare(first, True, listed, own_ref, (own_ref, sibling_ref), lists_ref, weight_ref, tools)
    build_targets([part_of(own_ref, tiles, axis) for axis in range(3)], middle, tools[3], target_ref)
    total_ref[...] = jnp.zeros(total_ref.shape, jnp.float32)
    copy.wait()
    accumulate(tiles, tools[1], tools[5], target_ref, tools[4], total_ref)


def halves(speed, even, half):
    first, last = (speed[:half], speed[half:])
    return jnp.where(even, last, first), jnp.where(even, first, last)


def first_finish(
    listed, own_ref, pair, forwarded, total_in, target_ref, weight_own_ref, speed_ref, *refs
):
    total_ref, lists_ref, weight_ref, place_out, speed_out, sibling_out, beside_out, *scratch = refs
    *tools, sums_ref = scratch
    tiles = own_ref.shape[0] // tools[0].shape[0]
    half = tiles // 2
    middle, copy = prepare(True, False, listed, own_ref, far_blocks(pair, forwarded, own_ref.shape[0]), lists_ref, weight_ref, tools)
    copy.wait()
    accumulate(tiles, tools[1], tools[5], target_ref, tools[4], total_ref)
    places, speeds = advance(
        middle,
        [part_of(own_ref, tiles, axis) for axis in range(3)],
        [part_of(speed_ref, tiles, axis) for axis in range(3)],
        weight_own_ref[:tiles, :],
        total_ref,
        sums_ref,
    )
    even = device_index() % 2 == 0
    for axis in range(3):
        strip = slice(axis * tiles, (axis + 1) * tiles)
        place_out[strip, :] = places[axis]
        speed_out[strip, :] = speeds[axis]
        sibling_out[strip, :] = places[axis]
        beside_out[strip, :] = places[axis]
        strip = slice(3 * tiles + axis * half, 3 * tiles + (axis + 1) * half)
        sibling_out[strip, :], beside_out[strip, :] = halves(speeds[axis], even, half)


def second_finish(
    total_tiles,
    cuts_ref,
    own_ref,
    pair,
    forwarded,
    total_in,
    target_ref,
    weight_own_ref,
    speed_ref,
    sibling_ref,
    lists_ref,
    weight_ref,
    total_ref,
    state_ref,
    sibling_out,
    beside_out,
    out_ref,
    *scratch
):
    *tools, sums_ref, pool_ref = scratch
    tiles = own_ref.shape[0] // 3
    half = tiles // 2
    beside = pair[: 3 * (tiles + half), :]
    blocks = far_blocks(pair, forwarded, beside.shape[0])
    middle, copy = prepare(False, False, None, own_ref, blocks, lists_ref, weight_ref, tools)
    copy.wait()
    accumulate(tiles, tools[1], tools[5], target_ref, tools[4], total_ref)
    place_own = [part_of(own_ref, tiles, axis) for axis in range(3)]
    speed_own = [part_of(speed_ref, tiles, axis) for axis in range(3)]
    places, speeds = advance(middle, place_own, speed_own, weight_own_ref[:tiles, :], total_ref, sums_ref)
    even = device_index() % 2 == 0
    for row, value in enumerate(places + speeds):
        state_ref[row] = value
        strip = slice(row * half, (row + 1) * half)
        sibling_out[strip, :], beside_out[strip, :] = halves(value, even, half)
    lower, upper = ([], [])
    for row in range(6):
        if row < 3:
            sides = [part_of(ref, tiles, row) for ref in (sibling_ref, beside)]
            low_sides, high_sides = ([side[tiles - half :] for side in sides], [side[:half] for side in sides])
        else:
            strip = slice(3 * tiles + (row - 3) * half, 3 * tiles + (row - 2) * half)
            low_sides = high_sides = [ref[strip, :] for ref in (sibling_ref, beside)]
        lower.append(jnp.where(even, low_sides[1], low_sides[0]))
        upper.append(jnp.where(even, high_sides[0], high_sides[1]))
    place_rows(0, total_tiles, cuts_ref, lower, place_own + speed_own, upper, pool_ref, out_ref)


def place_rows(step, total_tiles, cuts_ref, lower, own, upper, pool_ref, out_ref):
    tiles, slots = own[0].shape
    half = tiles // 2
    capacity = out_ref.shape[1]
    device = device_index()
    last = cuts_ref.shape[1] - 1
    first_tile = cuts_ref[step, device]
    next_tile = jnp.where(device == last, total_tiles, cuts_ref[step, jnp.minimum(device + 1, last)])
    owned = next_tile - first_tile
    start = first_tile - (device * tiles - half)
    filled = lax.broadcasted_iota(jnp.int32, (capacity, slots), 0) < owned
    for row in range(6):
        pool_ref[row, :half, :] = lower[row]
        pool_ref[row, half : half + tiles, :] = own[row]
        pool_ref[row, half + tiles : 2 * tiles, :] = upper[row]
    for row in range(6):
        out_ref[row] = jnp.where(filled, pool_ref[row, pl.ds(start, capacity), :], 0.0)


def third_kernel(total_tiles, cuts_ref, sibling_ref, own_ref, beside_ref, out_ref, pool_ref):
    half = own_ref.shape[1] // 2
    even = device_index() % 2 == 0
    lower, upper = ([], [])
    for row in range(6):
        sibling, beside = (part_of(sibling_ref, half, row), part_of(beside_ref, half, row))
        lower.append(jnp.where(even, beside, sibling))
        upper.append(jnp.where(even, sibling, beside))
    place_rows(1, total_tiles, cuts_ref, lower, [own_ref[row] for row in range(6)], upper, pool_ref, out_ref)


def far(value):
    return pltpu.with_memory_space_constraint(value, pltpu.HBM)


def near(value):
    return pltpu.with_memory_space_constraint(value, pltpu.VMEM)


def body(particles, occupancy, neighbours, curve_cuts):
    tiles, _, slots = particles.shape
    listed = neighbours.shape[1]
    total_tiles = tiles * lax.axis_size(AXES)
    half = tiles // 2
    capacity = 2 * tiles
    near_rows = round_up(2 * tiles + 1, 8)
    far_rows = round_up((reach + 1) * tiles + 1, 8)
    list_rows = round_up(tiles + 2, 8)
    vmem = pl.BlockSpec(memory_space=pltpu.VMEM)
    smem = pl.BlockSpec(memory_space=pltpu.SMEM)

    def held(*sizes, dtype=jnp.float32):
        return pltpu.VMEM(sizes, dtype)

    def call(kernel, name, outs, ins, scratch, flops=0, aliases=None):
        held_ins = [far(value) if kind is smem else near(value) for kind, value in ins]
        return pl.pallas_call(
            kernel,
            out_shape=outs,
            in_specs=[kind for kind, _ in ins],
            out_specs=[vmem] * len(outs),
            scratch_shapes=scratch,
            input_output_aliases=aliases or {},
            compiler_params=pltpu.CompilerParams(vmem_limit_bytes=vmem_limit),
            cost_estimate=pl.CostEstimate(flops=flops, bytes_accessed=1 << 20, transcendentals=0),
            name=name,
        )(*held_ins)

    def tools(rows, kinds):
        return [
            pltpu.VMEM((kinds, rows, slots), jnp.float32),
            pltpu.SMEM((list_rows, lanes), jnp.int32),
            pltpu.SemaphoreType.DMA,
            pltpu.VMEM((rows * feature_rows, lanes), jnp.float32),
            pltpu.VMEM((rows, 8, lanes), jnp.float32),
            pltpu.VMEM((rows, feature_rows, lanes), jnp.bfloat16),
        ]

    packed, speed = pl.pallas_call(
        functools.partial(pack_kernel, total_tiles),
        out_shape=(held(4 * tiles, slots), held(3 * tiles, slots)),
        in_specs=[vmem, smem, vmem],
        out_specs=(vmem, vmem),
        compiler_params=pltpu.CompilerParams(vmem_limit_bytes=vmem_limit),
        name="pack",
    )(far(particles), far(occupancy), far(neighbours))
    pool_scratch = pltpu.VMEM((6, round_up(capacity + tiles, 8), slots), jnp.float32)
    sums_scratch = pltpu.VMEM((4, round_up(tiles, 8), lanes), jnp.float32)
    blocks = lanes // block_rows
    totals = held(tiles * blocks + 1, 4, block_rows, lanes)
    targets = held(tiles * blocks + 1, block_rows, feature_rows, dtype=jnp.bfloat16)
    lists = held(list_rows, lanes, dtype=jnp.int32)
    edge = 3 * tiles + 3 * half
    work = 1 << 32

    sibling = swapped(packed, 0)
    pair = swapped(jnp.concatenate([packed, sibling], axis=0), 1)
    total, target, near_lists, near_weight = call(
        functools.partial(begin, listed, True),
        "first_near",
        [totals, targets, lists, held(near_rows, slots)],
        [(vmem, packed), (vmem, sibling)],
        tools(near_rows, 4),
        work,
    )
    pair, near_weight = lax.optimization_barrier((pair, near_weight))
    forwarded = swapped(pair, 0)
    total, far_lists, far_weight, place, speed, sibling, beside = call(
        functools.partial(first_finish, listed),
        "first_far",
        [totals, lists, held(far_rows, slots), held(3 * tiles, slots), held(3 * tiles, slots), held(edge, slots), held(edge, slots)],
        [(vmem, value) for value in (packed, pair, forwarded, total, target, near_weight, speed)],
        tools(far_rows, 4) + [sums_scratch],
        work,
        {3: 0},
    )
    sibling = swapped(sibling, 0)
    pair = swapped(jnp.concatenate([beside, sibling[: 3 * tiles]], axis=0), 1)
    total, target = call(
        functools.partial(begin, listed, False),
        "second_near",
        [totals, targets],
        [(vmem, value) for value in (place, sibling, near_lists, near_weight)],
        tools(near_rows, 3),
        work,
    )
    pair, target = lax.optimization_barrier((pair, target))
    forwarded = swapped(pair, 0)
    _, state, sibling, beside, after_first = call(
        functools.partial(second_finish, total_tiles),
        "second_far",
        [
            totals,
            held(6, tiles, slots),
            held(6 * half, slots),
            held(6 * half, slots),
            jax.ShapeDtypeStruct((6, capacity, slots), jnp.float32),
        ],
        [(smem, curve_cuts)]
        + [
            (vmem, value)
            for value in (place, pair, forwarded, total, target, near_weight, speed, sibling, far_lists, far_weight)
        ],
        tools(far_rows, 3) + [sums_scratch, pool_scratch],
        work,
        {4: 0},
    )
    (after_second,) = call(
        functools.partial(third_kernel, total_tiles),
        "place",
        [jax.ShapeDtypeStruct((6, capacity, slots), jnp.float32)],
        [(smem, curve_cuts), (vmem, swapped(sibling, 0)), (vmem, state), (vmem, swapped(beside, 1, wrap=False))],
        [pool_scratch],
    )
    return (jnp.transpose(after_first, (1, 0, 2)), jnp.transpose(after_second, (1, 0, 2)))


def solution(mesh):
    in_specs = (P(AXES, None, None), P(AXES), P(AXES, None), P())
    out_specs = (P(AXES, None, None), P(AXES, None, None))
    return jax.shard_map(body, mesh=mesh, in_specs=in_specs, out_specs=out_specs, check_vma=False)
```

profile of v0, /device:TPU:8, one launch (start us, length us, event | category | flops | bytes accessed | tf_op | source)
XLA Modules:
  0.0 57.9 jit_solution(2165242370445419152)
XLA Ops:
  0.6 0.8 %pack.1 = (f32[48,128]{1,0:T(8,128)S(1)}, f32[36,128]{1,0:T(8,128)S(1)}) custom-call(f32[12,6,128]{2,1,0:T(8,128)} %particles_ref.1, s32[12]{0:T(128)} %occupancy_ref.1, s32[12,16]{1,0:T(8,128)} %neighbours_ref.1), custom_call_target="tpu_custom_call" | custom-call | tf_op jit(solution)/shard_map/pack/pallas_call | solution.py:479
  1.5 0.1 collective-permute-start
  1.6 1.2 %collective-permute-done.refs_1_ = f32[48,128]{1,0:T(8,128)S(1)} collective-permute-done((f32[48,128]{1,0:T(8,128)S(1)}, f32[48,128]{1,0:T(8,128)S(1)}, u32[]{:S(2)}, u32[]{:S(2)}) %collective-permute-start) | collective-permute-done | bytes 24608 | tf_op jit(solution)/shard_map/ppermute | solution.py:32
  2.7 2.1 %collective-permute-start.1 = (f32[96,128]{1,0:T(8,128)S(1)}, f32[96,128]{1,0:T(8,128)S(1)}, u32[]{:S(2)}, u32[]{:S(2)}) collective-permute-start(f32[96,128]{1,0:T(8,128)S(1)} %pad_maximum_fusion), channel_id=1, source_target_pairs={{1,2},{2,1},{3,4},{4,3},{5,6},{6,5},{7,8},{8,7},{9,10},{10,9},{11,... | collective-permute-start | bytes 147464 | tf_op jit(solution)/shard_map/ppermute | solution.py:32
  4.8 10.0 %first_near.1 = (f32[49,4,32,128]{3,2,1,0:T(8,128)S(1)}, bf16[49,32,32]{2,1,0:T(8,128)(2,1)S(1)}, s32[16,128]{1,0:T(8,128)S(1)}, f32[32,128]{1,0:T(8,128)S(1)}) custom-call(f32[48,128]{1,0:T(8,128)S(1)} %get-tuple-element.24.refs_0_.own_ref, f32[48,128]{1,0:T(8,128)S(1)} %collective-permute-done.refs_1_), custom_call_target="tpu_custom_call" | custom-call | flops 4294967296 | bytes 1048576 | tf_op jit(solution)/shard_map/first_near/pallas_call | solution.py:457
  14.8 0.0 collective-permute-done.1.pair
  14.8 0.1 collective-permute-start.2
  14.9 1.2 %collective-permute-done.2.forwarded = f32[96,128]{1,0:T(8,128)S(1)} collective-permute-done((f32[96,128]{1,0:T(8,128)S(1)}, f32[96,128]{1,0:T(8,128)S(1)}, u32[]{:S(2)}, u32[]{:S(2)}) %collective-permute-start.2) | collective-permute-done | bytes 49184 | tf_op jit(solution)/shard_map/ppermute | solution.py:32
  16.1 10.5 %first_far.1 = (f32[49,4,32,128]{3,2,1,0:T(8,128)S(1)}, s32[16,128]{1,0:T(8,128)S(1)}, f32[40,128]{1,0:T(8,128)S(1)}, f32[36,128]{1,0:T(8,128)S(1)}, f32[36,128]...) custom-call(f32[48,128]{1,0:T(8,128)S(1)} %get-tuple-element.24.refs_0_.own_ref, ...), custom_call_target="tpu_custom_call", output_to_operand_aliasing={{0}: (3, {})} | custom-call | flops 4294967296 | bytes 1048576 | tf_op jit(solution)/shard_map/first_far/pallas_call | solution.py:457
  26.7 0.1 collective-permute-start.3
  26.8 1.2 %collective-permute-done.3.refs_1_.sibling_ref = f32[54,128]{1,0:T(8,128)S(1)} collective-permute-done((f32[54,128]{1,0:T(8,128)S(1)}, f32[54,128]{1,0:T(8,128)S(1)}, u32[]{:S(2)}, u32[]{:S(2)}) %collective-permute-start.3) | collective-permute-done | bytes 27680 | tf_op jit(solution)/shard_map/ppermute | solution.py:32
  28.0 0.1 collective-permute-start.4
  28.0 9.3 %second_near.1 = (f32[49,4,32,128]{3,2,1,0:T(8,128)S(1)}, bf16[49,32,32]{2,1,0:T(8,128)(2,1)S(1)}) custom-call(f32[36,128]{1,0:T(8,128)S(1)} %get-tuple-element.31.refs_0_.own_ref, f32[54,128]{1,0:T(8,128)S(1)} %collective-permute-done.3.refs_1_.sibling_ref, s32[16,128]{1,0:T(8,128)S(1)} %get-tuple-element.34.refs_2_, ...), custom_call_target="tpu_custom_call" | custom-call | flops 4294967296 | bytes 1048576 | tf_op jit(solution)/shard_map/second_near/pallas_call | solution.py:457
  37.4 0.0 collective-permute-done.4.pair
  37.4 0.1 collective-permute-start.5
  37.5 1.2 %collective-permute-done.5.forwarded = f32[90,128]{1,0:T(8,128)S(1)} collective-permute-done((f32[90,128]{1,0:T(8,128)S(1)}, f32[90,128]{1,0:T(8,128)S(1)}, u32[]{:S(2)}, u32[]{:S(2)}) %collective-permute-start.5) | collective-permute-done | bytes 46112 | tf_op jit(solution)/shard_map/ppermute | solution.py:32
  38.7 10.8 %second_far.1 = (f32[49,4,32,128]{3,2,1,0:T(8,128)S(1)}, f32[6,12,128]{2,1,0:T(8,128)S(1)}, f32[36,128]{1,0:T(8,128)S(1)}, f32[36,128]{1,0:T(8,128)S(1)}, f32[6,24,128]{2,1,0:T(8,128)}) custom-call(s32[2,32]{1,0:T(2,128)} %cuts_ref.3, f32[36,128]{1,0:T(8,128)S(1)} %get-tuple-element.31.refs_0_.own_ref, ...), custom_call_target="tpu_custom_call", output_to_operand_aliasing={{0}: (4, {})} | custom-call | flops 4294967296 | bytes 1048576 | tf_op jit(solution)/shard_map/second_far/pallas_call | solution.py:457
  49.5 0.1 collective-permute-start.6
  49.5 3.0 %collective-permute-start.7 = (f32[36,128]{1,0:T(8,128)S(1)}, f32[36,128]{1,0:T(8,128)S(1)}, u32[]{:S(2)}, u32[]{:S(2)}) collective-permute-start(f32[36,128]{1,0:T(8,128)S(1)} %get-tuple-element.45), channel_id=1, source_target_pairs={{1,2},{2,1},{3,4},{4,3},{5,6},{6,5},{7,8},{8,7},{9,10},{10,9},{11,... | collective-permute-start | bytes 55304 | tf_op jit(solution)/shard_map/ppermute | solution.py:32
  52.6 0.0 collective-permute-done.6.sibling_ref
  52.6 4.0 %collective-permute-done.7.beside_ref = f32[36,128]{1,0:T(8,128)S(1)} collective-permute-done((f32[36,128]{1,0:T(8,128)S(1)}, f32[36,128]{1,0:T(8,128)S(1)}, u32[]{:S(2)}, u32[]{:S(2)}) %collective-permute-start.7) | collective-permute-done | bytes 18464 | tf_op jit(solution)/shard_map/ppermute | solution.py:32
  56.6 1.3 %place.1 = f32[6,24,128]{2,1,0:T(8,128)} custom-call(s32[2,32]{1,0:T(2,128)} %cuts_ref.3, f32[36,128]{1,0:T(8,128)S(1)} %collective-permute-done.6.sibling_ref, f32[6,12,128]{2,1,0:T(8,128)S(1)} %get-tuple-element.44.own_ref, f32[36,128]{1,0:T(8,128)S(1)} %collective-permute-done.7.beside_ref), custom_call_target="tpu_custom_call" | custom-call | bytes 1048576 | tf_op jit(solution)/shard_map/place/pallas_call | solution.py:457
  (3 shorter events, 0.0 us)
Async XLA Ops:
  1.5 1.3 %collective-permute-start = (f32[48,128]{1,0:T(8,128)S(1)}, f32[48,128]{1,0:T(8,128)S(1)}, u32[]{:S(2)}, u32[]{:S(2)}) collective-permute-start(f32[48,128]{1,0:T(8,128)S(1)} %get-tuple-element.24.refs_0_.own_ref), channel_id=1, source_target_pairs={{0,1},{1,0},{2,3},{3,2},{4,5},{5,4},{6,7},{7,6},{8,9},{9,8},{10,11... | collective-permute-start | bytes 73736 | tf_op jit(solution)/shard_map/ppermute | solution.py:32
  2.7 12.1 %collective-permute-start.1 = (f32[96,128]{1,0:T(8,128)S(1)}, f32[96,128]{1,0:T(8,128)S(1)}, u32[]{:S(2)}, u32[]{:S(2)}) collective-permute-start(f32[96,128]{1,0:T(8,128)S(1)} %pad_maximum_fusion), channel_id=1, source_target_pairs={{1,2},{2,1},{3,4},{4,3},{5,6},{6,5},{7,8},{8,7},{9,10},{10,9},{11,... | collective-permute-start | bytes 147464 | tf_op jit(solution)/shard_map/ppermute | solution.py:32
  14.8 1.3 %collective-permute-start.2 = (f32[96,128]{1,0:T(8,128)S(1)}, f32[96,128]{1,0:T(8,128)S(1)}, u32[]{:S(2)}, u32[]{:S(2)}) collective-permute-start(f32[96,128]{1,0:T(8,128)S(1)} %collective-permute-done.1.pair), channel_id=1, source_target_pairs={{0,1},{1,0},{2,3},{3,2},{4,5},{5,4},{6,7},{7,6},{8,9},{9,8},{10,11... | collective-permute-start | bytes 147464 | tf_op jit(solution)/shard_map/ppermute | solution.py:32
  26.7 1.3 %collective-permute-start.3 = (f32[54,128]{1,0:T(8,128)S(1)}, f32[54,128]{1,0:T(8,128)S(1)}, u32[]{:S(2)}, u32[]{:S(2)}) collective-permute-start(f32[54,128]{1,0:T(8,128)S(1)} %get-tuple-element.33), channel_id=1, source_target_pairs={{0,1},{1,0},{2,3},{3,2},{4,5},{5,4},{6,7},{7,6},{8,9},{9,8},{10,11... | collective-permute-start | bytes 82952 | tf_op jit(solution)/shard_map/ppermute | solution.py:32
  28.0 9.4 %collective-permute-start.4 = (f32[90,128]{1,0:T(8,128)S(1)}, f32[90,128]{1,0:T(8,128)S(1)}, u32[]{:S(2)}, u32[]{:S(2)}) collective-permute-start(f32[90,128]{1,0:T(8,128)S(1)} %pad_maximum_fusion.1), channel_id=1, source_target_pairs={{1,2},{2,1},{3,4},{4,3},{5,6},{6,5},{7,8},{8,7},{9,10},{10,9},{11,... | collective-permute-start | bytes 138248 | tf_op jit(solution)/shard_map/ppermute | solution.py:32
  37.4 1.3 %collective-permute-start.5 = (f32[90,128]{1,0:T(8,128)S(1)}, f32[90,128]{1,0:T(8,128)S(1)}, u32[]{:S(2)}, u32[]{:S(2)}) collective-permute-start(f32[90,128]{1,0:T(8,128)S(1)} %collective-permute-done.4.pair), channel_id=1, source_target_pairs={{0,1},{1,0},{2,3},{3,2},{4,5},{5,4},{6,7},{7,6},{8,9},{9,8},{10,11... | collective-permute-start | bytes 138248 | tf_op jit(solution)/shard_map/ppermute | solution.py:32
  49.5 3.1 %collective-permute-start.6 = (f32[36,128]{1,0:T(8,128)S(1)}, f32[36,128]{1,0:T(8,128)S(1)}, u32[]{:S(2)}, u32[]{:S(2)}) collective-permute-start(f32[36,128]{1,0:T(8,128)S(1)} %get-tuple-element.43), channel_id=1, source_target_pairs={{0,1},{1,0},{2,3},{3,2},{4,5},{5,4},{6,7},{7,6},{8,9},{9,8},{10,11... | collective-permute-start | bytes 55304 | tf_op jit(solution)/shard_map/ppermute | solution.py:32
  49.5 7.0 %collective-permute-start.7 = (f32[36,128]{1,0:T(8,128)S(1)}, f32[36,128]{1,0:T(8,128)S(1)}, u32[]{:S(2)}, u32[]{:S(2)}) collective-permute-start(f32[36,128]{1,0:T(8,128)S(1)} %get-tuple-element.45), channel_id=1, source_target_pairs={{1,2},{2,1},{3,4},{4,3},{5,6},{6,5},{7,8},{8,7},{9,10},{10,9},{11,... | collective-permute-start | bytes 55304 | tf_op jit(solution)/shard_map/ppermute | solution.py:32
where the time goes:
time: 58.9 us; the launch traced here: 57.9 us
  Pallas kernels  42.8 us (73%)
  waiting for transfers between devices  8.81 us (15%)
  starting transfers between devices  5.52 us (9%)
  between operations  0.76 us (1%)
    pallas_call x5, Pallas kernels, call(): pl.pallas_call(kernel, out_shape=outs, in_specs=[kind for kind, _ in ins]...  42 us
    ppermute x8, waiting for transfers between devices, swapped(): return lax.ppermute(value, AXES, pairs)  8.81 us
    ppermute x8, starting transfers between devices, swapped(): return lax.ppermute(value, AXES, pairs)  5.52 us
  transfers between devices with their start and end apart: 8, of which 5 were waited for; matrix products, arithmetic and copies ran while one was open for 0% of the time, Pallas kernels for 33%

commit v1 on v0

--- a/solution.py
+++ b/solution.py
@@ -14,11 +14,11 @@
 time_step = 0.5
 reach = 2
 chunk = 4
-units = 12
+units = 8
 feature_rows = 32
 far_norm = 1e36
 lanes = 128
-block_rows = 32
+block_rows = 64
 vmem_limit = 16 << 20
 
 

time: 58.9 us -> 57.9 us (0.983)
  the two profiles are of different devices: /device:TPU:8 before, /device:TPU:1 now
where the time goes in v1:
time: 57.9 us; the launch traced here: 58.6 us
  Pallas kernels  36.3 us (63%)
  starting transfers between devices  14.7 us (25%)
  waiting for transfers between devices  6.93 us (12%)
  between operations  0.72 us (1%)
    pallas_call x5, Pallas kernels, call(): pl.pallas_call(kernel, out_shape=outs, in_specs=[kind for kind, _ in ins]...  35.4 us
    ppermute x8, starting transfers between devices, swapped(): return lax.ppermute(value, AXES, pairs)  14.7 us
    ppermute x8, waiting for transfers between devices, swapped(): return lax.ppermute(value, AXES, pairs)  6.93 us
  transfers between devices with their start and end apart: 8, of which 5 were waited for; matrix products, arithmetic and copies ran while one was open for 0% of the time, Pallas kernels for 27%

profile of v1, /device:TPU:1, one launch (start us, length us, event | category | flops | bytes accessed | tf_op | source)
XLA Modules:
  0.0 58.6 jit_solution(11088646483329707970)
XLA Ops:
  0.6 0.8 %pack.1 = (f32[48,128]{1,0:T(8,128)S(1)}, f32[36,128]{1,0:T(8,128)S(1)}) custom-call(f32[12,6,128]{2,1,0:T(8,128)} %particles_ref.1, s32[12]{0:T(128)} %occupancy_ref.1, s32[12,16]{1,0:T(8,128)} %neighbours_ref.1), custom_call_target="tpu_custom_call" | custom-call | tf_op jit(solution)/shard_map/pack/pallas_call | solution.py:479
  1.5 0.1 collective-permute-start
  1.6 1.1 %collective-permute-done.refs_1_ = f32[48,128]{1,0:T(8,128)S(1)} collective-permute-done((f32[48,128]{1,0:T(8,128)S(1)}, f32[48,128]{1,0:T(8,128)S(1)}, u32[]{:S(2)}, u32[]{:S(2)}) %collective-permute-start) | collective-permute-done | bytes 24608 | tf_op jit(solution)/shard_map/ppermute | solution.py:32
  2.7 2.6 %collective-permute-start.1 = (f32[96,128]{1,0:T(8,128)S(1)}, f32[96,128]{1,0:T(8,128)S(1)}, u32[]{:S(2)}, u32[]{:S(2)}) collective-permute-start(f32[96,128]{1,0:T(8,128)S(1)} %pad_maximum_fusion), channel_id=1, source_target_pairs={{1,2},{2,1},{3,4},{4,3},{5,6},{6,5},{7,8},{8,7},{9,10},{10,9},{11,... | collective-permute-start | bytes 147464 | tf_op jit(solution)/shard_map/ppermute | solution.py:32
  5.3 8.2 %first_near.1 = (f32[25,4,64,128]{3,2,1,0:T(8,128)S(1)}, bf16[25,64,32]{2,1,0:T(8,128)(2,1)S(1)}, s32[16,128]{1,0:T(8,128)S(1)}, f32[32,128]{1,0:T(8,128)S(1)}) custom-call(f32[48,128]{1,0:T(8,128)S(1)} %get-tuple-element.24.refs_0_.own_ref, f32[48,128]{1,0:T(8,128)S(1)} %collective-permute-done.refs_1_), custom_call_target="tpu_custom_call" | custom-call | flops 4294967296 | bytes 1048576 | tf_op jit(solution)/shard_map/first_near/pallas_call | solution.py:457
  13.6 0.0 collective-permute-done.1.pair
  13.6 5.4 %collective-permute-start.2 = (f32[96,128]{1,0:T(8,128)S(1)}, f32[96,128]{1,0:T(8,128)S(1)}, u32[]{:S(2)}, u32[]{:S(2)}) collective-permute-start(f32[96,128]{1,0:T(8,128)S(1)} %collective-permute-done.1.pair), channel_id=1, source_target_pairs={{0,1},{1,0},{2,3},{3,2},{4,5},{5,4},{6,7},{7,6},{8,9},{9,8},{10,11... | collective-permute-start | bytes 147464 | tf_op jit(solution)/shard_map/ppermute | solution.py:32
  19.0 0.9 %collective-permute-done.2.forwarded = f32[96,128]{1,0:T(8,128)S(1)} collective-permute-done((f32[96,128]{1,0:T(8,128)S(1)}, f32[96,128]{1,0:T(8,128)S(1)}, u32[]{:S(2)}, u32[]{:S(2)}) %collective-permute-start.2) | collective-permute-done | bytes 49184 | tf_op jit(solution)/shard_map/ppermute | solution.py:32
  19.8 9.1 %first_far.1 = (f32[25,4,64,128]{3,2,1,0:T(8,128)S(1)}, s32[16,128]{1,0:T(8,128)S(1)}, f32[40,128]{1,0:T(8,128)S(1)}, f32[36,128]{1,0:T(8,128)S(1)}, f32[36,128]...) custom-call(f32[48,128]{1,0:T(8,128)S(1)} %get-tuple-element.24.refs_0_.own_ref, ...), custom_call_target="tpu_custom_call", output_to_operand_aliasing={{0}: (3, {})} | custom-call | flops 4294967296 | bytes 1048576 | tf_op jit(solution)/shard_map/first_far/pallas_call | solution.py:457
  28.9 1.6 %collective-permute-start.3 = (f32[54,128]{1,0:T(8,128)S(1)}, f32[54,128]{1,0:T(8,128)S(1)}, u32[]{:S(2)}, u32[]{:S(2)}) collective-permute-start(f32[54,128]{1,0:T(8,128)S(1)} %get-tuple-element.33), channel_id=1, source_target_pairs={{0,1},{1,0},{2,3},{3,2},{4,5},{5,4},{6,7},{7,6},{8,9},{9,8},{10,11... | collective-permute-start | bytes 82952 | tf_op jit(solution)/shard_map/ppermute | solution.py:32
  30.5 0.9 %collective-permute-done.3.refs_1_.sibling_ref = f32[54,128]{1,0:T(8,128)S(1)} collective-permute-done((f32[54,128]{1,0:T(8,128)S(1)}, f32[54,128]{1,0:T(8,128)S(1)}, u32[]{:S(2)}, u32[]{:S(2)}) %collective-permute-start.3) | collective-permute-done | bytes 27680 | tf_op jit(solution)/shard_map/ppermute | solution.py:32
  31.4 0.1 collective-permute-start.4
  31.4 7.4 %second_near.1 = (f32[25,4,64,128]{3,2,1,0:T(8,128)S(1)}, bf16[25,64,32]{2,1,0:T(8,128)(2,1)S(1)}) custom-call(f32[36,128]{1,0:T(8,128)S(1)} %get-tuple-element.31.refs_0_.own_ref, f32[54,128]{1,0:T(8,128)S(1)} %collective-permute-done.3.refs_1_.sibling_ref, s32[16,128]{1,0:T(8,128)S(1)} %get-tuple-element.34.refs_2_, ...), custom_call_target="tpu_custom_call" | custom-call | flops 4294967296 | bytes 1048576 | tf_op jit(solution)/shard_map/second_near/pallas_call | solution.py:457
  38.8 0.0 collective-permute-done.4.pair
  38.9 1.6 %collective-permute-start.5 = (f32[90,128]{1,0:T(8,128)S(1)}, f32[90,128]{1,0:T(8,128)S(1)}, u32[]{:S(2)}, u32[]{:S(2)}) collective-permute-start(f32[90,128]{1,0:T(8,128)S(1)} %collective-permute-done.4.pair), channel_id=1, source_target_pairs={{0,1},{1,0},{2,3},{3,2},{4,5},{5,4},{6,7},{7,6},{8,9},{9,8},{10,11... | collective-permute-start | bytes 138248 | tf_op jit(solution)/shard_map/ppermute | solution.py:32
  40.4 0.9 %collective-permute-done.5.forwarded = f32[90,128]{1,0:T(8,128)S(1)} collective-permute-done((f32[90,128]{1,0:T(8,128)S(1)}, f32[90,128]{1,0:T(8,128)S(1)}, u32[]{:S(2)}, u32[]{:S(2)}) %collective-permute-start.5) | collective-permute-done | bytes 46112 | tf_op jit(solution)/shard_map/ppermute | solution.py:32
  41.3 9.4 %second_far.1 = (f32[25,4,64,128]{3,2,1,0:T(8,128)S(1)}, f32[6,12,128]{2,1,0:T(8,128)S(1)}, f32[36,128]{1,0:T(8,128)S(1)}, f32[36,128]{1,0:T(8,128)S(1)}, f32[6,24,128]{2,1,0:T(8,128)}) custom-call(s32[2,32]{1,0:T(2,128)} %cuts_ref.3, f32[36,128]{1,0:T(8,128)S(1)} %get-tuple-element.31.refs_0_.own_ref, ...), custom_call_target="tpu_custom_call", output_to_operand_aliasing={{0}: (4, {})} | custom-call | flops 4294967296 | bytes 1048576 | tf_op jit(solution)/shard_map/second_far/pallas_call | solution.py:457
  50.7 1.5 %collective-permute-start.6 = (f32[36,128]{1,0:T(8,128)S(1)}, f32[36,128]{1,0:T(8,128)S(1)}, u32[]{:S(2)}, u32[]{:S(2)}) collective-permute-start(f32[36,128]{1,0:T(8,128)S(1)} %get-tuple-element.43), channel_id=1, source_target_pairs={{0,1},{1,0},{2,3},{3,2},{4,5},{5,4},{6,7},{7,6},{8,9},{9,8},{10,11... | collective-permute-start | bytes 55304 | tf_op jit(solution)/shard_map/ppermute | solution.py:32
  52.2 1.9 %collective-permute-start.7 = (f32[36,128]{1,0:T(8,128)S(1)}, f32[36,128]{1,0:T(8,128)S(1)}, u32[]{:S(2)}, u32[]{:S(2)}) collective-permute-start(f32[36,128]{1,0:T(8,128)S(1)} %get-tuple-element.45), channel_id=1, source_target_pairs={{1,2},{2,1},{3,4},{4,3},{5,6},{6,5},{7,8},{8,7},{9,10},{10,9},{11,... | collective-permute-start | bytes 55304 | tf_op jit(solution)/shard_map/ppermute | solution.py:32
  54.1 0.0 collective-permute-done.6.sibling_ref
  54.1 3.2 %collective-permute-done.7.beside_ref = f32[36,128]{1,0:T(8,128)S(1)} collective-permute-done((f32[36,128]{1,0:T(8,128)S(1)}, f32[36,128]{1,0:T(8,128)S(1)}, u32[]{:S(2)}, u32[]{:S(2)}) %collective-permute-start.7) | collective-permute-done | bytes 18464 | tf_op jit(solution)/shard_map/ppermute | solution.py:32
  57.3 1.3 %place.1 = f32[6,24,128]{2,1,0:T(8,128)} custom-call(s32[2,32]{1,0:T(2,128)} %cuts_ref.3, f32[36,128]{1,0:T(8,128)S(1)} %collective-permute-done.6.sibling_ref, f32[6,12,128]{2,1,0:T(8,128)S(1)} %get-tuple-element.44.own_ref, f32[36,128]{1,0:T(8,128)S(1)} %collective-permute-done.7.beside_ref), custom_call_target="tpu_custom_call" | custom-call | bytes 1048576 | tf_op jit(solution)/shard_map/place/pallas_call | solution.py:457
  (3 shorter events, 0.0 us)
Async XLA Ops:
  1.5 1.3 %collective-permute-start = (f32[48,128]{1,0:T(8,128)S(1)}, f32[48,128]{1,0:T(8,128)S(1)}, u32[]{:S(2)}, u32[]{:S(2)}) collective-permute-start(f32[48,128]{1,0:T(8,128)S(1)} %get-tuple-element.24.refs_0_.own_ref), channel_id=1, source_target_pairs={{0,1},{1,0},{2,3},{3,2},{4,5},{5,4},{6,7},{7,6},{8,9},{9,8},{10,11... | collective-permute-start | bytes 73736 | tf_op jit(solution)/shard_map/ppermute | solution.py:32
  2.7 10.9 %collective-permute-start.1 = (f32[96,128]{1,0:T(8,128)S(1)}, f32[96,128]{1,0:T(8,128)S(1)}, u32[]{:S(2)}, u32[]{:S(2)}) collective-permute-start(f32[96,128]{1,0:T(8,128)S(1)} %pad_maximum_fusion), channel_id=1, source_target_pairs={{1,2},{2,1},{3,4},{4,3},{5,6},{6,5},{7,8},{8,7},{9,10},{10,9},{11,... | collective-permute-start | bytes 147464 | tf_op jit(solution)/shard_map/ppermute | solution.py:32
  13.6 6.2 %collective-permute-start.2 = (f32[96,128]{1,0:T(8,128)S(1)}, f32[96,128]{1,0:T(8,128)S(1)}, u32[]{:S(2)}, u32[]{:S(2)}) collective-permute-start(f32[96,128]{1,0:T(8,128)S(1)} %collective-permute-done.1.pair), channel_id=1, source_target_pairs={{0,1},{1,0},{2,3},{3,2},{4,5},{5,4},{6,7},{7,6},{8,9},{9,8},{10,11... | collective-permute-start | bytes 147464 | tf_op jit(solution)/shard_map/ppermute | solution.py:32
  28.9 2.4 %collective-permute-start.3 = (f32[54,128]{1,0:T(8,128)S(1)}, f32[54,128]{1,0:T(8,128)S(1)}, u32[]{:S(2)}, u32[]{:S(2)}) collective-permute-start(f32[54,128]{1,0:T(8,128)S(1)} %get-tuple-element.33), channel_id=1, source_target_pairs={{0,1},{1,0},{2,3},{3,2},{4,5},{5,4},{6,7},{7,6},{8,9},{9,8},{10,11... | collective-permute-start | bytes 82952 | tf_op jit(solution)/shard_map/ppermute | solution.py:32
  31.4 7.5 %collective-permute-start.4 = (f32[90,128]{1,0:T(8,128)S(1)}, f32[90,128]{1,0:T(8,128)S(1)}, u32[]{:S(2)}, u32[]{:S(2)}) collective-permute-start(f32[90,128]{1,0:T(8,128)S(1)} %pad_maximum_fusion.1), channel_id=1, source_target_pairs={{1,2},{2,1},{3,4},{4,3},{5,6},{6,5},{7,8},{8,7},{9,10},{10,9},{11,... | collective-permute-start | bytes 138248 | tf_op jit(solution)/shard_map/ppermute | solution.py:32
  38.9 2.4 %collective-permute-start.5 = (f32[90,128]{1,0:T(8,128)S(1)}, f32[90,128]{1,0:T(8,128)S(1)}, u32[]{:S(2)}, u32[]{:S(2)}) collective-permute-start(f32[90,128]{1,0:T(8,128)S(1)} %collective-permute-done.4.pair), channel_id=1, source_target_pairs={{0,1},{1,0},{2,3},{3,2},{4,5},{5,4},{6,7},{7,6},{8,9},{9,8},{10,11... | collective-permute-start | bytes 138248 | tf_op jit(solution)/shard_map/ppermute | solution.py:32
  50.7 3.5 %collective-permute-start.6 = (f32[36,128]{1,0:T(8,128)S(1)}, f32[36,128]{1,0:T(8,128)S(1)}, u32[]{:S(2)}, u32[]{:S(2)}) collective-permute-start(f32[36,128]{1,0:T(8,128)S(1)} %get-tuple-element.43), channel_id=1, source_target_pairs={{0,1},{1,0},{2,3},{3,2},{4,5},{5,4},{6,7},{7,6},{8,9},{9,8},{10,11... | collective-permute-start | bytes 55304 | tf_op jit(solution)/shard_map/ppermute | solution.py:32
  52.2 5.1 %collective-permute-start.7 = (f32[36,128]{1,0:T(8,128)S(1)}, f32[36,128]{1,0:T(8,128)S(1)}, u32[]{:S(2)}, u32[]{:S(2)}) collective-permute-start(f32[36,128]{1,0:T(8,128)S(1)} %get-tuple-element.45), channel_id=1, source_target_pairs={{1,2},{2,1},{3,4},{4,3},{5,6},{6,5},{7,8},{8,7},{9,10},{10,9},{11,... | collective-permute-start | bytes 55304 | tf_op jit(solution)/shard_map/ppermute | solution.py:32

commit v2 on v1

--- a/solution.py
+++ b/solution.py
@@ -125,8 +125,9 @@
     return feature_ref[tile * feature_rows : (tile + 1) * feature_rows, :]
 
 
-def build_sources(places, middle, weight, feature_ref, moment_ref, source_ref):
+def build_sources(first, places, middle, weight, feature_ref, moment_ref, source_ref):
     rows = weight.shape[0]
+    moment_rows = moment_ref.reshape(moment_ref.shape[0] * 8, lanes)
     ones = jnp.ones_like(weight)
     zeros = jnp.zeros_like(weight)
     features = []
@@ -134,7 +135,7 @@
     for axis in range(3):
         value = weight * (places[axis] - middle[axis])
         norm = norm + value * value
-        moment_ref.reshape(rows * 8, lanes)[pl.ds(axis, rows, 8), :] = value
+        moment_rows[pl.ds(first * 8 + axis, rows, 8), :] = value
         high, mid, low = pieces(value, 3)
         features += [high, high, mid, mid, high, low]
     features += pieces(jnp.where(weight > 0.5, norm, far_norm), 3) + [ones] * 3
@@ -142,7 +143,7 @@
     for row, value in enumerate(features):
         feature_ref[pl.ds(row, rows, feature_rows), :] = value
     for tile in range(rows):
-        source_ref[tile] = feature_of(feature_ref, tile).astype(jnp.bfloat16)
+        source_ref[first + tile] = feature_of(feature_ref, tile).astype(jnp.bfloat16)
 
 
 def build_targets(own_place, middle, feature_ref, target_ref):
@@ -282,6 +283,7 @@
 
 def prepare(first, near_pair, listed, own_ref, blocks, lists_ref, weight_ref, tools):
     planes, scalars, copy_sem, feature_ref, moment_ref, source_ref = tools
+    first_row = own_ref.shape[0] // planes.shape[0] if near_pair else 0
     tiles = own_ref.shape[0] // planes.shape[0]
     if not first:
         copy = pltpu.make_async_copy(lists_ref, scalars, copy_sem)
@@ -298,20 +300,36 @@
         copy.start()
         weight_ref[...] = weights_of(aux, listed)
     middle = middles([part_of(own_ref, tiles, axis) for axis in range(3)])
-    build_sources([planes[axis] for axis in range(3)], middle, weight_ref[...], feature_ref, moment_ref, source_ref)
+    places = [planes[axis, first_row:, :] for axis in range(3)]
+    build_sources(first_row, places, middle, weight_ref[first_row:, :], feature_ref, moment_ref, source_ref)
     return middle, copy
 
 
+def alone(listed, first, *refs):
+    if first:
+        own_ref, total_ref, target_ref, moment_ref, source_ref, feature_ref = refs
+        tiles = own_ref.shape[0] // 4
+        weight = weights_of(part_of(own_ref, tiles, 3), listed)
+    else:
+        own_ref, weight_ref, total_ref, target_ref, moment_ref, source_ref, feature_ref = refs
+        tiles = own_ref.shape[0] // 3
+        weight = weight_ref[:tiles, :]
+    own_place = [part_of(own_ref, tiles, axis) for axis in range(3)]
+    middle = middles(own_place)
+    total_ref[...] = jnp.zeros(total_ref.shape, jnp.float32)
+    build_targets(own_place, middle, feature_ref, target_ref)
+    build_sources(0, own_place, middle, weight, feature_ref, moment_ref, source_ref)
+
+
 def begin(listed, first, *refs):
+    own_ref, sibling_ref, target_ref, _, _, _, *refs = refs
     if first:
-        own_ref, sibling_ref, total_ref, target_ref, lists_ref, weight_ref, *scratch = refs
+        total_ref, moment_ref, source_ref, lists_ref, weight_ref, *scratch = refs
     else:
-        own_ref, sibling_ref, lists_ref, weight_ref, total_ref, target_ref, *scratch = refs
-    tools = scratch
+        lists_ref, weight_ref, total_ref, moment_ref, source_ref, *scratch = refs
+    tools = scratch + [moment_ref, source_ref]
     tiles = own_ref.shape[0] // tools[0].shape[0]
-    middle, copy = prepare(first, True, listed, own_ref, (own_ref, sibling_ref), lists_ref, weight_ref, tools)
-    build_targets([part_of(own_ref, tiles, axis) for axis in range(3)], middle, tools[3], target_ref)
-    total_ref[...] = jnp.zeros(total_ref.shape, jnp.float32)
+    _, copy = prepare(first, True, listed, own_ref, (own_ref, sibling_ref), lists_ref, weight_ref, tools)
     copy.wait()
     accumulate(tiles, tools[1], tools[5], target_ref, tools[4], total_ref)
 
@@ -466,14 +484,21 @@
             name=name,
         )(*held_ins)
 
+    def moments(rows):
+        return held(rows, 8, lanes)
+
+    def sources(rows):
+        return held(rows, feature_rows, lanes, dtype=jnp.bfloat16)
+
+    def features(rows):
+        return pltpu.VMEM((rows * feature_rows, lanes), jnp.float32)
+
     def tools(rows, kinds):
         return [
             pltpu.VMEM((kinds, rows, slots), jnp.float32),
             pltpu.SMEM((list_rows, lanes), jnp.int32),
             pltpu.SemaphoreType.DMA,
-            pltpu.VMEM((rows * feature_rows, lanes), jnp.float32),
-            pltpu.VMEM((rows, 8, lanes), jnp.float32),
-            pltpu.VMEM((rows, feature_rows, lanes), jnp.bfloat16),
+            features(rows),
         ]
 
     packed, speed = pl.pallas_call(
@@ -495,13 +520,23 @@
 
     sibling = swapped(packed, 0)
     pair = swapped(jnp.concatenate([packed, sibling], axis=0), 1)
-    total, target, near_lists, near_weight = call(
+    carried = [totals, moments(near_rows), sources(near_rows)]
+    total, target, moment, source = call(
+        functools.partial(alone, listed, True),
+        "first_alone",
+        [totals, targets, *carried[1:]],
+        [(vmem, packed)],
+        [features(round_up(tiles, 8))],
+        1 << 22,
+    )
+    total, _, _, near_lists, near_weight = call(
         functools.partial(begin, listed, True),
         "first_near",
-        [totals, targets, lists, held(near_rows, slots)],
-        [(vmem, packed), (vmem, sibling)],
+        carried + [lists, held(near_rows, slots)],
+        [(vmem, value) for value in (packed, sibling, target, total, moment, source)],
         tools(near_rows, 4),
         work,
+        {3: 0, 4: 1, 5: 2},
     )
     pair, near_weight = lax.optimization_barrier((pair, near_weight))
     forwarded = swapped(pair, 0)
@@ -510,21 +545,30 @@
         "first_far",
         [totals, lists, held(far_rows, slots), held(3 * tiles, slots), held(3 * tiles, slots), held(edge, slots), held(edge, slots)],
         [(vmem, value) for value in (packed, pair, forwarded, total, target, near_weight, speed)],
-        tools(far_rows, 4) + [sums_scratch],
+        tools(far_rows, 4) + [moments(far_rows), sources(far_rows), sums_scratch],
         work,
         {3: 0},
     )
     sibling = swapped(sibling, 0)
     pair = swapped(jnp.concatenate([beside, sibling[: 3 * tiles]], axis=0), 1)
-    total, target = call(
+    total, target, moment, source = call(
+        functools.partial(alone, listed, False),
+        "second_alone",
+        [totals, targets, *carried[1:]],
+        [(vmem, place), (vmem, near_weight)],
+        [features(round_up(tiles, 8))],
+        1 << 22,
+    )
+    total, _, _ = call(
         functools.partial(begin, listed, False),
         "second_near",
-        [totals, targets],
-        [(vmem, value) for value in (place, sibling, near_lists, near_weight)],
+        carried,
+        [(vmem, value) for value in (place, sibling, target, total, moment, source, near_lists, near_weight)],
         tools(near_rows, 3),
         work,
-    )
-    pair, target = lax.optimization_barrier((pair, target))
+        {3: 0, 4: 1, 5: 2},
+    )
+    pair, total = lax.optimization_barrier((pair, total))
     forwarded = swapped(pair, 0)
     _, state, sibling, beside, after_first = call(
         functools.partial(second_finish, total_tiles),
@@ -541,15 +585,17 @@
             (vmem, value)
             for value in (place, pair, forwarded, total, target, near_weight, speed, sibling, far_lists, far_weight)
         ],
-        tools(far_rows, 3) + [sums_scratch, pool_scratch],
+        tools(far_rows, 3) + [moments(far_rows), sources(far_rows), sums_scratch, pool_scratch],
         work,
         {4: 0},
     )
+    beside = swapped(beside, 1, wrap=False)
+    sibling = swapped(sibling, 0)
     (after_second,) = call(
         functools.partial(third_kernel, total_tiles),
         "place",
         [jax.ShapeDtypeStruct((6, capacity, slots), jnp.float32)],
-        [(smem, curve_cuts), (vmem, swapped(sibling, 0)), (vmem, state), (vmem, swapped(beside, 1, wrap=False))],
+        [(smem, curve_cuts), (vmem, sibling), (vmem, state), (vmem, beside)],
         [pool_scratch],
     )
     return (jnp.transpose(after_first, (1, 0, 2)), jnp.transpose(after_second, (1, 0, 2)))

time: 57.9 us -> 56.1 us (0.969); the launches traced: 58.6 us -> 55.7 us
  waiting for transfers between devices: 6.93 us -> 4.1 us
  starting transfers between devices: 14.7 us -> 14 us
    ppermute x8, waiting for transfers between devices: 6.93 us -> 4.1 us  [swapped(): return lax.ppermute(value, AXES, pairs)]
    ppermute x8, starting transfers between devices: 14.7 us -> 14 us  [swapped(): return lax.ppermute(value, AXES, pairs)]
    pallas_call x5 -> x7, Pallas kernels: 35.4 us -> 36 us  [call(): pl.pallas_call(kernel, out_shape=outs, in_specs=[kind for kind, _ in ins]...]
  transfers between devices with their start and end apart: 8 -> 8, of which waited for: 5 -> 5; matrix products, arithmetic and copies ran while one was open for 0% -> 0% of each run, Pallas kernels for 27% -> 29%
where the time goes in v2:
time: 56.1 us; the launch traced here: 55.7 us
  Pallas kernels  36.8 us (66%)
  starting transfers between devices  14 us (25%)
  waiting for transfers between devices  4.1 us (7%)
  between operations  0.73 us (1%)
    pallas_call x7, Pallas kernels, call(): pl.pallas_call(kernel, out_shape=outs, in_specs=[kind for kind, _ in ins]...  36 us
    ppermute x8, starting transfers between devices, swapped(): return lax.ppermute(value, AXES, pairs)  14 us
    ppermute x8, waiting for transfers between devices, swapped(): return lax.ppermute(value, AXES, pairs)  4.1 us
  transfers between devices with their start and end apart: 8, of which 5 were waited for; matrix products, arithmetic and copies ran while one was open for 0% of the time, Pallas kernels for 29%

profile of v2, /device:TPU:1, one launch (start us, length us, event | category | flops | bytes accessed | tf_op | source)
XLA Modules:
  0.0 55.7 jit_solution(6878946571604894164)
XLA Ops:
  0.6 0.8 %pack.1 = (f32[48,128]{1,0:T(8,128)S(1)}, f32[36,128]{1,0:T(8,128)S(1)}) custom-call(f32[12,6,128]{2,1,0:T(8,128)} %particles_ref.1, s32[12]{0:T(128)} %occupancy_ref.1, s32[12,16]{1,0:T(8,128)} %neighbours_ref.1), custom_call_target="tpu_custom_call" | custom-call | tf_op jit(solution)/shard_map/pack/pallas_call | solution.py:504
  1.5 0.1 collective-permute-start
  1.6 0.6 %first_alone.1 = (f32[25,4,64,128]{3,2,1,0:T(8,128)S(1)}, bf16[25,64,32]{2,1,0:T(8,128)(2,1)S(1)}, f32[32,8,128]{2,1,0:T(8,128)S(1)}, bf16[32,32,128]{2,1,0:T(8,128)(2,1)S(1)}) custom-call(f32[48,128]{1,0:T(8,128)S(1)} %get-tuple-element.30.refs_0_.own_ref), custom_call_target="tpu_custom_call" | custom-call | flops 4194304 | bytes 1048576 | tf_op jit(solution)/shard_map/first_alone/pallas_call | solution.py:475
  2.3 0.5 collective-permute-done.refs_1_
  2.7 2.6 %collective-permute-start.1 = (f32[96,128]{1,0:T(8,128)S(1)}, f32[96,128]{1,0:T(8,128)S(1)}, u32[]{:S(2)}, u32[]{:S(2)}) collective-permute-start(f32[96,128]{1,0:T(8,128)S(1)} %pad_maximum_fusion), channel_id=1, source_target_pairs={{1,2},{2,1},{3,4},{4,3},{5,6},{6,5},{7,8},{8,7},{9,10},{10,9},{11,... | collective-permute-start | bytes 147464 | tf_op jit(solution)/shard_map/ppermute | solution.py:32
  5.3 7.8 %first_near.1 = (f32[25,4,64,128]{3,2,1,0:T(8,128)S(1)}, f32[32,8,128]{2,1,0:T(8,128)S(1)}, bf16[32,32,128]{2,1,0:T(8,128)(2,1)S(1)}, s32[16,128]{1,0:T(8,128)S(1)}, f32[32,128]{1,0:T(8,128)S(1)}) custom-call(f32[48,128]{1,0:T(8,128)S(1)} %get-tuple-element.30.refs_0_.own_ref, ...), custom_call_target="tpu_custom_call", output_to_operand_aliasing={{0}: (3, {}), {1}: (4, {}), {2}: (5, {})} | custom-call | flops 4294967296 | bytes 1048576 | tf_op jit(solution)/shard_map/first_near/pallas_call | solution.py:475
  13.1 0.0 collective-permute-done.1.pair
  13.1 4.8 %collective-permute-start.2 = (f32[96,128]{1,0:T(8,128)S(1)}, f32[96,128]{1,0:T(8,128)S(1)}, u32[]{:S(2)}, u32[]{:S(2)}) collective-permute-start(f32[96,128]{1,0:T(8,128)S(1)} %collective-permute-done.1.pair), channel_id=1, source_target_pairs={{0,1},{1,0},{2,3},{3,2},{4,5},{5,4},{6,7},{7,6},{8,9},{9,8},{10,11... | collective-permute-start | bytes 147464 | tf_op jit(solution)/shard_map/ppermute | solution.py:32
  17.9 0.9 %collective-permute-done.2.forwarded = f32[96,128]{1,0:T(8,128)S(1)} collective-permute-done((f32[96,128]{1,0:T(8,128)S(1)}, f32[96,128]{1,0:T(8,128)S(1)}, u32[]{:S(2)}, u32[]{:S(2)}) %collective-permute-start.2) | collective-permute-done | bytes 49184 | tf_op jit(solution)/shard_map/ppermute | solution.py:32
  18.8 9.1 %first_far.1 = (f32[25,4,64,128]{3,2,1,0:T(8,128)S(1)}, s32[16,128]{1,0:T(8,128)S(1)}, f32[40,128]{1,0:T(8,128)S(1)}, f32[36,128]{1,0:T(8,128)S(1)}, f32[36,128]...) custom-call(f32[48,128]{1,0:T(8,128)S(1)} %get-tuple-element.30.refs_0_.own_ref, ...), custom_call_target="tpu_custom_call", output_to_operand_aliasing={{0}: (3, {})} | custom-call | flops 4294967296 | bytes 1048576 | tf_op jit(solution)/shard_map/first_far/pallas_call | solution.py:475
  27.9 1.0 %collective-permute-start.3 = (f32[54,128]{1,0:T(8,128)S(1)}, f32[54,128]{1,0:T(8,128)S(1)}, u32[]{:S(2)}, u32[]{:S(2)}) collective-permute-start(f32[54,128]{1,0:T(8,128)S(1)} %get-tuple-element.42), channel_id=1, source_target_pairs={{0,1},{1,0},{2,3},{3,2},{4,5},{5,4},{6,7},{7,6},{8,9},{9,8},{10,11... | collective-permute-start | bytes 82952 | tf_op jit(solution)/shard_map/ppermute | solution.py:32
  28.9 0.6 %second_alone.1 = (f32[25,4,64,128]{3,2,1,0:T(8,128)S(1)}, bf16[25,64,32]{2,1,0:T(8,128)(2,1)S(1)}, f32[32,8,128]{2,1,0:T(8,128)S(1)}, bf16[32,32,128]{2,1,0:T(8,128)(2,1)S(1)}) custom-call(f32[36,128]{1,0:T(8,128)S(1)} %get-tuple-element.40.refs_0_.own_ref, f32[32,128]{1,0:T(8,128)S(1)} %get-tuple-element.38.weight_own_ref.refs_1_.refs_7_), custom_call_target="tpu_custom_call" | custom-call | flops 4194304 | bytes 1048576 | tf_op jit(solution)/shard_map/second_alone/pallas_call | solution.py:475
  29.5 0.2 collective-permute-done.3.refs_1_.sibling_ref
  29.8 0.1 collective-permute-start.4
  29.8 7.2 %second_near.1 = (f32[25,4,64,128]{3,2,1,0:T(8,128)S(1)}, f32[32,8,128]{2,1,0:T(8,128)S(1)}, bf16[32,32,128]{2,1,0:T(8,128)(2,1)S(1)}) custom-call(f32[36,128]{1,0:T(8,128)S(1)} %get-tuple-element.40.refs_0_.own_ref, f32[54,128]{1,0:T(8,128)S(1)} %collective-permute-done.3.refs_1_.sibling_ref, ...), custom_call_target="tpu_custom_call", output_to_operand_aliasing={{0}: (3, {}), {1}: (4, {}), {2}: (5, {})} | custom-call | flops 4294967296 | bytes 1048576 | tf_op jit(solution)/shard_map/second_near/pallas_call | solution.py:475
  37.1 0.0 collective-permute-done.4.pair
  37.1 1.0 %collective-permute-start.5 = (f32[90,128]{1,0:T(8,128)S(1)}, f32[90,128]{1,0:T(8,128)S(1)}, u32[]{:S(2)}, u32[]{:S(2)}) collective-permute-start(f32[90,128]{1,0:T(8,128)S(1)} %collective-permute-done.4.pair), channel_id=1, source_target_pairs={{0,1},{1,0},{2,3},{3,2},{4,5},{5,4},{6,7},{7,6},{8,9},{9,8},{10,11... | collective-permute-start | bytes 138248 | tf_op jit(solution)/shard_map/ppermute | solution.py:32
  38.1 0.9 %collective-permute-done.5.forwarded = f32[90,128]{1,0:T(8,128)S(1)} collective-permute-done((f32[90,128]{1,0:T(8,128)S(1)}, f32[90,128]{1,0:T(8,128)S(1)}, u32[]{:S(2)}, u32[]{:S(2)}) %collective-permute-start.5) | collective-permute-done | bytes 46112 | tf_op jit(solution)/shard_map/ppermute | solution.py:32
  39.0 9.3 %second_far.1 = (f32[25,4,64,128]{3,2,1,0:T(8,128)S(1)}, f32[6,12,128]{2,1,0:T(8,128)S(1)}, f32[36,128]{1,0:T(8,128)S(1)}, f32[36,128]{1,0:T(8,128)S(1)}, f32[6,24,128]{2,1,0:T(8,128)}) custom-call(s32[2,32]{1,0:T(2,128)} %cuts_ref.3, f32[36,128]{1,0:T(8,128)S(1)} %get-tuple-element.40.refs_0_.own_ref, ...), custom_call_target="tpu_custom_call", output_to_operand_aliasing={{0}: (4, {})} | custom-call | flops 4294967296 | bytes 1048576 | tf_op jit(solution)/shard_map/second_far/pallas_call | solution.py:475
  48.3 1.0 %collective-permute-start.6 = (f32[36,128]{1,0:T(8,128)S(1)}, f32[36,128]{1,0:T(8,128)S(1)}, u32[]{:S(2)}, u32[]{:S(2)}) collective-permute-start(f32[36,128]{1,0:T(8,128)S(1)} %get-tuple-element.55), channel_id=1, source_target_pairs={{0,1},{1,0},{2,3},{3,2},{4,5},{5,4},{6,7},{7,6},{8,9},{9,8},{10,11... | collective-permute-start | bytes 55304 | tf_op jit(solution)/shard_map/ppermute | solution.py:32
  49.2 3.4 %collective-permute-start.7 = (f32[36,128]{1,0:T(8,128)S(1)}, f32[36,128]{1,0:T(8,128)S(1)}, u32[]{:S(2)}, u32[]{:S(2)}) collective-permute-start(f32[36,128]{1,0:T(8,128)S(1)} %get-tuple-element.57), channel_id=1, source_target_pairs={{1,2},{2,1},{3,4},{4,3},{5,6},{6,5},{7,8},{8,7},{9,10},{10,9},{11,... | collective-permute-start | bytes 55304 | tf_op jit(solution)/shard_map/ppermute | solution.py:32
  52.7 0.0 collective-permute-done.6.sibling_ref
  52.7 1.6 %collective-permute-done.7.beside_ref = f32[36,128]{1,0:T(8,128)S(1)} collective-permute-done((f32[36,128]{1,0:T(8,128)S(1)}, f32[36,128]{1,0:T(8,128)S(1)}, u32[]{:S(2)}, u32[]{:S(2)}) %collective-permute-start.7) | collective-permute-done | bytes 18464 | tf_op jit(solution)/shard_map/ppermute | solution.py:32
  54.3 1.3 %place.1 = f32[6,24,128]{2,1,0:T(8,128)} custom-call(s32[2,32]{1,0:T(2,128)} %cuts_ref.3, f32[36,128]{1,0:T(8,128)S(1)} %collective-permute-done.6.sibling_ref, f32[6,12,128]{2,1,0:T(8,128)S(1)} %get-tuple-element.56.own_ref, f32[36,128]{1,0:T(8,128)S(1)} %collective-permute-done.7.beside_ref), custom_call_target="tpu_custom_call" | custom-call | bytes 1048576 | tf_op jit(solution)/shard_map/place/pallas_call | solution.py:475
  (3 shorter events, 0.0 us)
Async XLA Ops:
  1.5 1.3 %collective-permute-start = (f32[48,128]{1,0:T(8,128)S(1)}, f32[48,128]{1,0:T(8,128)S(1)}, u32[]{:S(2)}, u32[]{:S(2)}) collective-permute-start(f32[48,128]{1,0:T(8,128)S(1)} %get-tuple-element.30.refs_0_.own_ref), channel_id=1, source_target_pairs={{0,1},{1,0},{2,3},{3,2},{4,5},{5,4},{6,7},{7,6},{8,9},{9,8},{10,11... | collective-permute-start | bytes 73736 | tf_op jit(solution)/shard_map/ppermute | solution.py:32
  2.7 10.4 %collective-permute-start.1 = (f32[96,128]{1,0:T(8,128)S(1)}, f32[96,128]{1,0:T(8,128)S(1)}, u32[]{:S(2)}, u32[]{:S(2)}) collective-permute-start(f32[96,128]{1,0:T(8,128)S(1)} %pad_maximum_fusion), channel_id=1, source_target_pairs={{1,2},{2,1},{3,4},{4,3},{5,6},{6,5},{7,8},{8,7},{9,10},{10,9},{11,... | collective-permute-start | bytes 147464 | tf_op jit(solution)/shard_map/ppermute | solution.py:32
  13.1 5.7 %collective-permute-start.2 = (f32[96,128]{1,0:T(8,128)S(1)}, f32[96,128]{1,0:T(8,128)S(1)}, u32[]{:S(2)}, u32[]{:S(2)}) collective-permute-start(f32[96,128]{1,0:T(8,128)S(1)} %collective-permute-done.1.pair), channel_id=1, source_target_pairs={{0,1},{1,0},{2,3},{3,2},{4,5},{5,4},{6,7},{7,6},{8,9},{9,8},{10,11... | collective-permute-start | bytes 147464 | tf_op jit(solution)/shard_map/ppermute | solution.py:32
  27.9 1.8 %collective-permute-start.3 = (f32[54,128]{1,0:T(8,128)S(1)}, f32[54,128]{1,0:T(8,128)S(1)}, u32[]{:S(2)}, u32[]{:S(2)}) collective-permute-start(f32[54,128]{1,0:T(8,128)S(1)} %get-tuple-element.42), channel_id=1, source_target_pairs={{0,1},{1,0},{2,3},{3,2},{4,5},{5,4},{6,7},{7,6},{8,9},{9,8},{10,11... | collective-permute-start | bytes 82952 | tf_op jit(solution)/shard_map/ppermute | solution.py:32
  29.8 7.3 %collective-permute-start.4 = (f32[90,128]{1,0:T(8,128)S(1)}, f32[90,128]{1,0:T(8,128)S(1)}, u32[]{:S(2)}, u32[]{:S(2)}) collective-permute-start(f32[90,128]{1,0:T(8,128)S(1)} %pad_maximum_fusion.1), channel_id=1, source_target_pairs={{1,2},{2,1},{3,4},{4,3},{5,6},{6,5},{7,8},{8,7},{9,10},{10,9},{11,... | collective-permute-start | bytes 138248 | tf_op jit(solution)/shard_map/ppermute | solution.py:32
  37.1 1.9 %collective-permute-start.5 = (f32[90,128]{1,0:T(8,128)S(1)}, f32[90,128]{1,0:T(8,128)S(1)}, u32[]{:S(2)}, u32[]{:S(2)}) collective-permute-start(f32[90,128]{1,0:T(8,128)S(1)} %collective-permute-done.4.pair), channel_id=1, source_target_pairs={{0,1},{1,0},{2,3},{3,2},{4,5},{5,4},{6,7},{7,6},{8,9},{9,8},{10,11... | collective-permute-start | bytes 138248 | tf_op jit(solution)/shard_map/ppermute | solution.py:32
  48.3 4.4 %collective-permute-start.6 = (f32[36,128]{1,0:T(8,128)S(1)}, f32[36,128]{1,0:T(8,128)S(1)}, u32[]{:S(2)}, u32[]{:S(2)}) collective-permute-start(f32[36,128]{1,0:T(8,128)S(1)} %get-tuple-element.55), channel_id=1, source_target_pairs={{0,1},{1,0},{2,3},{3,2},{4,5},{5,4},{6,7},{7,6},{8,9},{9,8},{10,11... | collective-permute-start | bytes 55304 | tf_op jit(solution)/shard_map/ppermute | solution.py:32
  49.2 5.1 %collective-permute-start.7 = (f32[36,128]{1,0:T(8,128)S(1)}, f32[36,128]{1,0:T(8,128)S(1)}, u32[]{:S(2)}, u32[]{:S(2)}) collective-permute-start(f32[36,128]{1,0:T(8,128)S(1)} %get-tuple-element.57), channel_id=1, source_target_pairs={{1,2},{2,1},{3,4},{4,3},{5,6},{6,5},{7,8},{8,7},{9,10},{10,9},{11,... | collective-permute-start | bytes 55304 | tf_op jit(solution)/shard_map/ppermute | solution.py:32

commit v3 on v2

--- a/solution.py
+++ b/solution.py
@@ -369,8 +369,6 @@
 
 
 def second_finish(
-    total_tiles,
-    cuts_ref,
     own_ref,
     pair,
     forwarded,
@@ -378,17 +376,15 @@
     target_ref,
     weight_own_ref,
     speed_ref,
-    sibling_ref,
     lists_ref,
     weight_ref,
     total_ref,
     state_ref,
     sibling_out,
     beside_out,
-    out_ref,
     *scratch
 ):
-    *tools, sums_ref, pool_ref = scratch
+    *tools, sums_ref = scratch
     tiles = own_ref.shape[0] // 3
     half = tiles // 2
     beside = pair[: 3 * (tiles + half), :]
@@ -404,6 +400,15 @@
         state_ref[row] = value
         strip = slice(row * half, (row + 1) * half)
         sibling_out[strip, :], beside_out[strip, :] = halves(value, even, half)
+
+
+def first_place(total_tiles, cuts_ref, own_ref, speed_ref, sibling_ref, pair, out_ref, pool_ref):
+    tiles = own_ref.shape[0] // 3
+    half = tiles // 2
+    beside = pair[: 3 * (tiles + half), :]
+    place_own = [part_of(own_ref, tiles, axis) for axis in range(3)]
+    speed_own = [part_of(speed_ref, tiles, axis) for axis in range(3)]
+    even = device_index() % 2 == 0
     lower, upper = ([], [])
     for row in range(6):
         if row < 3:
@@ -570,24 +575,30 @@
     )
     pair, total = lax.optimization_barrier((pair, total))
     forwarded = swapped(pair, 0)
-    _, state, sibling, beside, after_first = call(
-        functools.partial(second_finish, total_tiles),
+    (after_first,) = call(
+        functools.partial(first_place, total_tiles),
+        "first_place",
+        [jax.ShapeDtypeStruct((6, capacity, slots), jnp.float32)],
+        [(smem, curve_cuts)] + [(vmem, value) for value in (place, speed, sibling, pair)],
+        [pool_scratch],
+        1 << 22,
+    )
+    _, state, sibling, beside = call(
+        second_finish,
         "second_far",
         [
             totals,
             held(6, tiles, slots),
             held(6 * half, slots),
             held(6 * half, slots),
-            jax.ShapeDtypeStruct((6, capacity, slots), jnp.float32),
         ],
-        [(smem, curve_cuts)]
-        + [
+        [
             (vmem, value)
-            for value in (place, pair, forwarded, total, target, near_weight, speed, sibling, far_lists, far_weight)
+            for value in (place, pair, forwarded, total, target, near_weight, speed, far_lists, far_weight)
         ],
-        tools(far_rows, 3) + [moments(far_rows), sources(far_rows), sums_scratch, pool_scratch],
+        tools(far_rows, 3) + [moments(far_rows), sources(far_rows), sums_scratch],
         work,
-        {4: 0},
+        {3: 0},
     )
     beside = swapped(beside, 1, wrap=False)
     sibling = swapped(sibling, 0)

time: 56.1 us -> 55.5 us (0.989)
  starting transfers between devices: 14 us -> 8.69 us
  Pallas kernels: 36.8 us -> 41.7 us
    ppermute x8, starting transfers between devices: 14 us -> 8.69 us  [swapped(): return lax.ppermute(value, AXES, pairs)]
    pallas_call x7 -> x8, Pallas kernels: 36 us -> 40.9 us  [call(): pl.pallas_call(kernel, out_shape=outs, in_specs=[kind for kind, _ in ins]...]
  transfers between devices with their start and end apart: 8 -> 8, of which waited for: 5 -> 5; matrix products, arithmetic and copies ran while one was open for 0% -> 0% of each run, Pallas kernels for 29% -> 37%
where the time goes in v3:
time: 55.5 us; the launch traced here: 54.9 us
  Pallas kernels  41.7 us (75%)
  starting transfers between devices  8.69 us (16%)
  waiting for transfers between devices  3.69 us (7%)
  between operations  0.75 us (1%)
    pallas_call x8, Pallas kernels, call(): pl.pallas_call(kernel, out_shape=outs, in_specs=[kind for kind, _ in ins]...  40.9 us
    ppermute x8, starting transfers between devices, swapped(): return lax.ppermute(value, AXES, pairs)  8.69 us
    ppermute x8, waiting for transfers between devices, swapped(): return lax.ppermute(value, AXES, pairs)  3.69 us
  transfers between devices with their start and end apart: 8, of which 5 were waited for; matrix products, arithmetic and copies ran while one was open for 0% of the time, Pallas kernels for 37%

profile of v3, /device:TPU:1, one launch (start us, length us, event | category | flops | bytes accessed | tf_op | source)
XLA Modules:
  0.0 54.9 jit_solution(13111064434169030485)
XLA Ops:
  0.6 0.8 %pack.1 = (f32[48,128]{1,0:T(8,128)S(1)}, f32[36,128]{1,0:T(8,128)S(1)}) custom-call(f32[12,6,128]{2,1,0:T(8,128)} %particles_ref.1, s32[12]{0:T(128)} %occupancy_ref.1, s32[12,16]{1,0:T(8,128)} %neighbours_ref.1), custom_call_target="tpu_custom_call" | custom-call | tf_op jit(solution)/shard_map/pack/pallas_call | solution.py:509
  1.5 0.1 collective-permute-start
  1.6 0.6 %first_alone.1 = (f32[25,4,64,128]{3,2,1,0:T(8,128)S(1)}, bf16[25,64,32]{2,1,0:T(8,128)(2,1)S(1)}, f32[32,8,128]{2,1,0:T(8,128)S(1)}, bf16[32,32,128]{2,1,0:T(8,128)(2,1)S(1)}) custom-call(f32[48,128]{1,0:T(8,128)S(1)} %get-tuple-element.29.refs_0_.own_ref), custom_call_target="tpu_custom_call" | custom-call | flops 4194304 | bytes 1048576 | tf_op jit(solution)/shard_map/first_alone/pallas_call | solution.py:480
  2.3 0.5 collective-permute-done.refs_1_
  2.7 2.6 %collective-permute-start.1 = (f32[96,128]{1,0:T(8,128)S(1)}, f32[96,128]{1,0:T(8,128)S(1)}, u32[]{:S(2)}, u32[]{:S(2)}) collective-permute-start(f32[96,128]{1,0:T(8,128)S(1)} %pad_maximum_fusion), channel_id=1, source_target_pairs={{1,2},{2,1},{3,4},{4,3},{5,6},{6,5},{7,8},{8,7},{9,10},{10,9},{11,... | collective-permute-start | bytes 147464 | tf_op jit(solution)/shard_map/ppermute | solution.py:32
  5.3 8.9 %first_near.1 = (f32[25,4,64,128]{3,2,1,0:T(8,128)S(1)}, f32[32,8,128]{2,1,0:T(8,128)S(1)}, bf16[32,32,128]{2,1,0:T(8,128)(2,1)S(1)}, s32[16,128]{1,0:T(8,128)S(1)}, f32[32,128]{1,0:T(8,128)S(1)}) custom-call(f32[48,128]{1,0:T(8,128)S(1)} %get-tuple-element.29.refs_0_.own_ref, ...), custom_call_target="tpu_custom_call", output_to_operand_aliasing={{0}: (3, {}), {1}: (4, {}), {2}: (5, {})} | custom-call | flops 4294967296 | bytes 1048576 | tf_op jit(solution)/shard_map/first_near/pallas_call | solution.py:480
  14.3 0.0 collective-permute-done.1.pair
  14.3 2.5 %collective-permute-start.2 = (f32[96,128]{1,0:T(8,128)S(1)}, f32[96,128]{1,0:T(8,128)S(1)}, u32[]{:S(2)}, u32[]{:S(2)}) collective-permute-start(f32[96,128]{1,0:T(8,128)S(1)} %collective-permute-done.1.pair), channel_id=1, source_target_pairs={{0,1},{1,0},{2,3},{3,2},{4,5},{5,4},{6,7},{7,6},{8,9},{9,8},{10,11... | collective-permute-start | bytes 147464 | tf_op jit(solution)/shard_map/ppermute | solution.py:32
  16.8 0.9 %collective-permute-done.2.forwarded = f32[96,128]{1,0:T(8,128)S(1)} collective-permute-done((f32[96,128]{1,0:T(8,128)S(1)}, f32[96,128]{1,0:T(8,128)S(1)}, u32[]{:S(2)}, u32[]{:S(2)}) %collective-permute-start.2) | collective-permute-done | bytes 49184 | tf_op jit(solution)/shard_map/ppermute | solution.py:32
  17.7 10.2 %first_far.1 = (f32[25,4,64,128]{3,2,1,0:T(8,128)S(1)}, s32[16,128]{1,0:T(8,128)S(1)}, f32[40,128]{1,0:T(8,128)S(1)}, f32[36,128]{1,0:T(8,128)S(1)}, f32[36,128]...) custom-call(f32[48,128]{1,0:T(8,128)S(1)} %get-tuple-element.29.refs_0_.own_ref, ...), custom_call_target="tpu_custom_call", output_to_operand_aliasing={{0}: (3, {})} | custom-call | flops 4294967296 | bytes 1048576 | tf_op jit(solution)/shard_map/first_far/pallas_call | solution.py:480
  27.9 0.1 collective-permute-start.3
  28.0 0.6 %second_alone.1 = (f32[25,4,64,128]{3,2,1,0:T(8,128)S(1)}, bf16[25,64,32]{2,1,0:T(8,128)(2,1)S(1)}, f32[32,8,128]{2,1,0:T(8,128)S(1)}, bf16[32,32,128]{2,1,0:T(8,128)(2,1)S(1)}) custom-call(f32[36,128]{1,0:T(8,128)S(1)} %get-tuple-element.39.refs_0_.own_ref, f32[32,128]{1,0:T(8,128)S(1)} %get-tuple-element.37.weight_own_ref.refs_1_.refs_7_), custom_call_target="tpu_custom_call" | custom-call | flops 4194304 | bytes 1048576 | tf_op jit(solution)/shard_map/second_alone/pallas_call | solution.py:480
  28.6 0.5 collective-permute-done.3.refs_1_.sibling_ref
  29.2 0.1 collective-permute-start.4
  29.3 8.5 %second_near.1 = (f32[25,4,64,128]{3,2,1,0:T(8,128)S(1)}, f32[32,8,128]{2,1,0:T(8,128)S(1)}, bf16[32,32,128]{2,1,0:T(8,128)(2,1)S(1)}) custom-call(f32[36,128]{1,0:T(8,128)S(1)} %get-tuple-element.39.refs_0_.own_ref, f32[54,128]{1,0:T(8,128)S(1)} %collective-permute-done.3.refs_1_.sibling_ref, ...), custom_call_target="tpu_custom_call", output_to_operand_aliasing={{0}: (3, {}), {1}: (4, {}), {2}: (5, {})} | custom-call | flops 4294967296 | bytes 1048576 | tf_op jit(solution)/shard_map/second_near/pallas_call | solution.py:480
  37.8 0.0 collective-permute-done.4.pair
  37.8 0.1 collective-permute-start.5
  37.9 1.2 %collective-permute-done.5.forwarded = f32[90,128]{1,0:T(8,128)S(1)} collective-permute-done((f32[90,128]{1,0:T(8,128)S(1)}, f32[90,128]{1,0:T(8,128)S(1)}, u32[]{:S(2)}, u32[]{:S(2)}) %collective-permute-start.5) | collective-permute-done | bytes 46112 | tf_op jit(solution)/shard_map/ppermute | solution.py:32
  39.1 9.3 %second_far.1 = (f32[25,4,64,128]{3,2,1,0:T(8,128)S(1)}, f32[6,12,128]{2,1,0:T(8,128)S(1)}, f32[36,128]{1,0:T(8,128)S(1)}, f32[36,128]{1,0:T(8,128)S(1)}) custom-call(f32[36,128]{1,0:T(8,128)S(1)} %get-tuple-element.39.refs_0_.own_ref, f32[90,128]{1,0:T(8,128)S(1)} %collective-permute-done.4.pair, ...), custom_call_target="tpu_custom_call", output_to_operand_aliasing={{0}: (3, {})} | custom-call | flops 4294967296 | bytes 1048576 | tf_op jit(solution)/shard_map/second_far/pallas_call | solution.py:480
  48.4 0.1 collective-permute-start.6
  48.4 3.2 %collective-permute-start.7 = (f32[36,128]{1,0:T(8,128)S(1)}, f32[36,128]{1,0:T(8,128)S(1)}, u32[]{:S(2)}, u32[]{:S(2)}) collective-permute-start(f32[36,128]{1,0:T(8,128)S(1)} %get-tuple-element.55), channel_id=1, source_target_pairs={{1,2},{2,1},{3,4},{4,3},{5,6},{6,5},{7,8},{8,7},{9,10},{10,9},{11,... | collective-permute-start | bytes 55304 | tf_op jit(solution)/shard_map/ppermute | solution.py:32
  51.6 1.4 %first_place.1 = f32[6,24,128]{2,1,0:T(8,128)} custom-call(s32[2,32]{1,0:T(2,128)} %cuts_ref.3, f32[36,128]{1,0:T(8,128)S(1)} %get-tuple-element.39.refs_0_.own_ref, f32[36,128]{1,0:T(8,128)S(1)} %get-tuple-element.40.speed_ref, f32[54,128]{1,0:T(8,128)S(1)} %collective-permute-done.3.refs_1_.sibling_ref, f32[90,128]{1,0:T(8,128)S(1)} %collective-permute-done.4.pair), custom_call_target="tpu_custom_call" | custom-call | flops 4194304 | bytes 1048576 | tf_op jit(solution)/shard_map/first_place/pallas_call | solution.py:480
  53.0 0.0 collective-permute-done.6.sibling_ref
  53.0 0.6 %collective-permute-done.7.beside_ref = f32[36,128]{1,0:T(8,128)S(1)} collective-permute-done((f32[36,128]{1,0:T(8,128)S(1)}, f32[36,128]{1,0:T(8,128)S(1)}, u32[]{:S(2)}, u32[]{:S(2)}) %collective-permute-start.7) | collective-permute-done | bytes 18464 | tf_op jit(solution)/shard_map/ppermute | solution.py:32
  53.5 1.3 %place.1 = f32[6,24,128]{2,1,0:T(8,128)} custom-call(s32[2,32]{1,0:T(2,128)} %cuts_ref.3, f32[36,128]{1,0:T(8,128)S(1)} %collective-permute-done.6.sibling_ref, f32[6,12,128]{2,1,0:T(8,128)S(1)} %get-tuple-element.54.own_ref, f32[36,128]{1,0:T(8,128)S(1)} %collective-permute-done.7.beside_ref), custom_call_target="tpu_custom_call" | custom-call | bytes 1048576 | tf_op jit(solution)/shard_map/place/pallas_call | solution.py:480
  (3 shorter events, 0.0 us)
Async XLA Ops:
  1.5 1.3 %collective-permute-start = (f32[48,128]{1,0:T(8,128)S(1)}, f32[48,128]{1,0:T(8,128)S(1)}, u32[]{:S(2)}, u32[]{:S(2)}) collective-permute-start(f32[48,128]{1,0:T(8,128)S(1)} %get-tuple-element.29.refs_0_.own_ref), channel_id=1, source_target_pairs={{0,1},{1,0},{2,3},{3,2},{4,5},{5,4},{6,7},{7,6},{8,9},{9,8},{10,11... | collective-permute-start | bytes 73736 | tf_op jit(solution)/shard_map/ppermute | solution.py:32
  2.7 11.5 %collective-permute-start.1 = (f32[96,128]{1,0:T(8,128)S(1)}, f32[96,128]{1,0:T(8,128)S(1)}, u32[]{:S(2)}, u32[]{:S(2)}) collective-permute-start(f32[96,128]{1,0:T(8,128)S(1)} %pad_maximum_fusion), channel_id=1, source_target_pairs={{1,2},{2,1},{3,4},{4,3},{5,6},{6,5},{7,8},{8,7},{9,10},{10,9},{11,... | collective-permute-start | bytes 147464 | tf_op jit(solution)/shard_map/ppermute | solution.py:32
  14.3 3.4 %collective-permute-start.2 = (f32[96,128]{1,0:T(8,128)S(1)}, f32[96,128]{1,0:T(8,128)S(1)}, u32[]{:S(2)}, u32[]{:S(2)}) collective-permute-start(f32[96,128]{1,0:T(8,128)S(1)} %collective-permute-done.1.pair), channel_id=1, source_target_pairs={{0,1},{1,0},{2,3},{3,2},{4,5},{5,4},{6,7},{7,6},{8,9},{9,8},{10,11... | collective-permute-start | bytes 147464 | tf_op jit(solution)/shard_map/ppermute | solution.py:32
  27.9 1.3 %collective-permute-start.3 = (f32[54,128]{1,0:T(8,128)S(1)}, f32[54,128]{1,0:T(8,128)S(1)}, u32[]{:S(2)}, u32[]{:S(2)}) collective-permute-start(f32[54,128]{1,0:T(8,128)S(1)} %get-tuple-element.41), channel_id=1, source_target_pairs={{0,1},{1,0},{2,3},{3,2},{4,5},{5,4},{6,7},{7,6},{8,9},{9,8},{10,11... | collective-permute-start | bytes 82952 | tf_op jit(solution)/shard_map/ppermute | solution.py:32
  29.2 8.6 %collective-permute-start.4 = (f32[90,128]{1,0:T(8,128)S(1)}, f32[90,128]{1,0:T(8,128)S(1)}, u32[]{:S(2)}, u32[]{:S(2)}) collective-permute-start(f32[90,128]{1,0:T(8,128)S(1)} %pad_maximum_fusion.1), channel_id=1, source_target_pairs={{1,2},{2,1},{3,4},{4,3},{5,6},{6,5},{7,8},{8,7},{9,10},{10,9},{11,... | collective-permute-start | bytes 138248 | tf_op jit(solution)/shard_map/ppermute | solution.py:32
  37.8 1.3 %collective-permute-start.5 = (f32[90,128]{1,0:T(8,128)S(1)}, f32[90,128]{1,0:T(8,128)S(1)}, u32[]{:S(2)}, u32[]{:S(2)}) collective-permute-start(f32[90,128]{1,0:T(8,128)S(1)} %collective-permute-done.4.pair), channel_id=1, source_target_pairs={{0,1},{1,0},{2,3},{3,2},{4,5},{5,4},{6,7},{7,6},{8,9},{9,8},{10,11... | collective-permute-start | bytes 138248 | tf_op jit(solution)/shard_map/ppermute | solution.py:32
  48.4 4.6 %collective-permute-start.6 = (f32[36,128]{1,0:T(8,128)S(1)}, f32[36,128]{1,0:T(8,128)S(1)}, u32[]{:S(2)}, u32[]{:S(2)}) collective-permute-start(f32[36,128]{1,0:T(8,128)S(1)} %get-tuple-element.53), channel_id=1, source_target_pairs={{0,1},{1,0},{2,3},{3,2},{4,5},{5,4},{6,7},{7,6},{8,9},{9,8},{10,11... | collective-permute-start | bytes 55304 | tf_op jit(solution)/shard_map/ppermute | solution.py:32
  48.4 5.1 %collective-permute-start.7 = (f32[36,128]{1,0:T(8,128)S(1)}, f32[36,128]{1,0:T(8,128)S(1)}, u32[]{:S(2)}, u32[]{:S(2)}) collective-permute-start(f32[36,128]{1,0:T(8,128)S(1)} %get-tuple-element.55), channel_id=1, source_target_pairs={{1,2},{2,1},{3,4},{4,3},{5,6},{6,5},{7,8},{8,7},{9,10},{10,9},{11,... | collective-permute-start | bytes 55304 | tf_op jit(solution)/shard_map/ppermute | solution.py:32

commit v4 on v3

--- a/solution.py
+++ b/solution.py
@@ -283,7 +283,7 @@
 
 def prepare(first, near_pair, listed, own_ref, blocks, lists_ref, weight_ref, tools):
     planes, scalars, copy_sem, feature_ref, moment_ref, source_ref = tools
-    first_row = own_ref.shape[0] // planes.shape[0] if near_pair else 0
+    first_row = own_ref.shape[0] // planes.shape[0] * (1 if near_pair else reach)
     tiles = own_ref.shape[0] // planes.shape[0]
     if not first:
         copy = pltpu.make_async_copy(lists_ref, scalars, copy_sem)
@@ -321,6 +321,21 @@
     build_sources(0, own_place, middle, weight, feature_ref, moment_ref, source_ref)
 
 
+def ahead(listed, first, *refs):
+    own_ref, pair, *refs = refs
+    *given, moment_ref, source_ref, feature_ref = refs
+    tiles = own_ref.shape[0] // (4 if first else 3)
+    first_rows = own_ref.shape[0] if first else 3 * (tiles + tiles // 2)
+    middle = middles([part_of(own_ref, tiles, axis) for axis in range(3)])
+    for index, block in enumerate((pair[:first_rows, :], pair[first_rows:, :])):
+        if first:
+            weight = weights_of(part_of(block, tiles, 3), listed)
+        else:
+            weight = given[0][index * tiles : (index + 1) * tiles, :]
+        places = [part_of(block, tiles, axis) for axis in range(3)]
+        build_sources(index * tiles, places, middle, weight, feature_ref, moment_ref, source_ref)
+
+
 def begin(listed, first, *refs):
     own_ref, sibling_ref, target_ref, _, _, _, *refs = refs
     if first:
@@ -340,10 +355,11 @@
 
 
 def first_finish(
-    listed, own_ref, pair, forwarded, total_in, target_ref, weight_own_ref, speed_ref, *refs
+    listed, own_ref, pair, forwarded, total_in, target_ref, weight_own_ref, speed_ref, moment_in, source_in, *refs
 ):
-    total_ref, lists_ref, weight_ref, place_out, speed_out, sibling_out, beside_out, *scratch = refs
-    *tools, sums_ref = scratch
+    total_ref, moment_ref, source_ref, lists_ref, weight_ref, place_out, speed_out, *refs = refs
+    sibling_out, beside_out, *tools, sums_ref = refs
+    tools += [moment_ref, source_ref]
     tiles = own_ref.shape[0] // tools[0].shape[0]
     half = tiles // 2
     middle, copy = prepare(True, False, listed, own_ref, far_blocks(pair, forwarded, own_ref.shape[0]), lists_ref, weight_ref, tools)
@@ -378,13 +394,18 @@
     speed_ref,
     lists_ref,
     weight_ref,
+    moment_in,
+    source_in,
     total_ref,
+    moment_ref,
+    source_ref,
     state_ref,
     sibling_out,
     beside_out,
     *scratch
 ):
     *tools, sums_ref = scratch
+    tools += [moment_ref, source_ref]
     tiles = own_ref.shape[0] // 3
     half = tiles // 2
     beside = pair[: 3 * (tiles + half), :]
@@ -545,14 +566,24 @@
     )
     pair, near_weight = lax.optimization_barrier((pair, near_weight))
     forwarded = swapped(pair, 0)
-    total, far_lists, far_weight, place, speed, sibling, beside = call(
+    far_carried = [totals, moments(far_rows), sources(far_rows)]
+    moment, source = call(
+        functools.partial(ahead, listed, True),
+        "first_ahead",
+        far_carried[1:],
+        [(vmem, packed), (vmem, pair)],
+        [features(round_up(tiles, 8))],
+        1 << 22,
+    )
+    total, _, _, far_lists, far_weight, place, speed, sibling, beside = call(
         functools.partial(first_finish, listed),
         "first_far",
-        [totals, lists, held(far_rows, slots), held(3 * tiles, slots), held(3 * tiles, slots), held(edge, slots), held(edge, slots)],
-        [(vmem, value) for value in (packed, pair, forwarded, total, target, near_weight, speed)],
-        tools(far_rows, 4) + [moments(far_rows), sources(far_rows), sums_scratch],
+        far_carried
+        + [lists, held(far_rows, slots), held(3 * tiles, slots), held(3 * tiles, slots), held(edge, slots), held(edge, slots)],
+        [(vmem, value) for value in (packed, pair, forwarded, total, target, near_weight, speed, moment, source)],
+        tools(far_rows, 4) + [sums_scratch],
         work,
-        {3: 0},
+        {3: 0, 7: 1, 8: 2},
     )
     sibling = swapped(sibling, 0)
     pair = swapped(jnp.concatenate([beside, sibling[: 3 * tiles]], axis=0), 1)
@@ -583,22 +614,30 @@
         [pool_scratch],
         1 << 22,
     )
-    _, state, sibling, beside = call(
+    moment, source = call(
+        functools.partial(ahead, listed, False),
+        "second_ahead",
+        far_carried[1:],
+        [(vmem, place), (vmem, pair), (vmem, far_weight)],
+        [features(round_up(tiles, 8))],
+        1 << 22,
+    )
+    _, _, _, state, sibling, beside = call(
         second_finish,
         "second_far",
-        [
-            totals,
+        far_carried
+        + [
             held(6, tiles, slots),
             held(6 * half, slots),
             held(6 * half, slots),
         ],
         [
             (vmem, value)
-            for value in (place, pair, forwarded, total, target, near_weight, speed, far_lists, far_weight)
+            for value in (place, pair, forwarded, total, target, near_weight, speed, far_lists, far_weight, moment, source)
         ],
-        tools(far_rows, 3) + [moments(far_rows), sources(far_rows), sums_scratch],
+        tools(far_rows, 3) + [sums_scratch],
         work,
-        {3: 0},
+        {3: 0, 9: 1, 10: 2},
     )
     beside = swapped(beside, 1, wrap=False)
     sibling = swapped(sibling, 0)

time: 55.5 us -> 57.2 us (1.031)
  starting transfers between devices: 8.69 us -> 15.1 us
  Pallas kernels: 41.7 us -> 38.8 us
  waiting for transfers between devices: 3.69 us -> 1.9 us
    ppermute x8, starting transfers between devices: 8.69 us -> 15.1 us  [swapped(): return lax.ppermute(value, AXES, pairs)]
    pallas_call x8 -> x10, Pallas kernels: 40.9 us -> 37.9 us  [call(): pl.pallas_call(kernel, out_shape=outs, in_specs=[kind for kind, _ in ins]...]
    ppermute x8, waiting for transfers between devices: 3.69 us -> 1.9 us  [swapped(): return lax.ppermute(value, AXES, pairs)]
  transfers between devices with their start and end apart: 8 -> 8, of which waited for: 5 -> 5; matrix products, arithmetic and copies ran while one was open for 0% -> 0% of each run, Pallas kernels for 37% -> 32%
where the time goes in v4:
time: 57.2 us; the launch traced here: 56.5 us
  Pallas kernels  38.8 us (68%)
  starting transfers between devices  15.1 us (26%)
  waiting for transfers between devices  1.9 us (3%)
  between operations  0.74 us (1%)
    pallas_call x10, Pallas kernels, call(): pl.pallas_call(kernel, out_shape=outs, in_specs=[kind for kind, _ in ins]...  37.9 us
    ppermute x8, starting transfers between devices, swapped(): return lax.ppermute(value, AXES, pairs)  15.1 us
    ppermute x8, waiting for transfers between devices, swapped(): return lax.ppermute(value, AXES, pairs)  1.9 us
  transfers between devices with their start and end apart: 8, of which 5 were waited for; matrix products, arithmetic and copies ran while one was open for 0% of the time, Pallas kernels for 32%

profile of v4, /device:TPU:1, one launch (start us, length us, event | category | flops | bytes accessed | tf_op | source)
XLA Modules:
  0.0 56.5 jit_solution(8244721672983928291)
XLA Ops:
  0.6 0.8 %pack.1 = (f32[48,128]{1,0:T(8,128)S(1)}, f32[36,128]{1,0:T(8,128)S(1)}) custom-call(f32[12,6,128]{2,1,0:T(8,128)} %particles_ref.1, s32[12]{0:T(128)} %occupancy_ref.1, s32[12,16]{1,0:T(8,128)} %neighbours_ref.1), custom_call_target="tpu_custom_call" | custom-call | tf_op jit(solution)/shard_map/pack/pallas_call | solution.py:530
  1.5 0.1 collective-permute-start
  1.6 0.6 %first_alone.1 = (f32[25,4,64,128]{3,2,1,0:T(8,128)S(1)}, bf16[25,64,32]{2,1,0:T(8,128)(2,1)S(1)}, f32[32,8,128]{2,1,0:T(8,128)S(1)}, bf16[32,32,128]{2,1,0:T(8,128)(2,1)S(1)}) custom-call(f32[48,128]{1,0:T(8,128)S(1)} %get-tuple-element.33.refs_0_.own_ref), custom_call_target="tpu_custom_call" | custom-call | flops 4194304 | bytes 1048576 | tf_op jit(solution)/shard_map/first_alone/pallas_call | solution.py:501
  2.3 0.5 collective-permute-done.refs_1_
  2.7 2.6 %collective-permute-start.1 = (f32[96,128]{1,0:T(8,128)S(1)}, f32[96,128]{1,0:T(8,128)S(1)}, u32[]{:S(2)}, u32[]{:S(2)}) collective-permute-start(f32[96,128]{1,0:T(8,128)S(1)} %pad_maximum_fusion), channel_id=1, source_target_pairs={{1,2},{2,1},{3,4},{4,3},{5,6},{6,5},{7,8},{8,7},{9,10},{10,9},{11,... | collective-permute-start | bytes 147464 | tf_op jit(solution)/shard_map/ppermute | solution.py:32
  5.3 7.8 %first_near.1 = (f32[25,4,64,128]{3,2,1,0:T(8,128)S(1)}, f32[32,8,128]{2,1,0:T(8,128)S(1)}, bf16[32,32,128]{2,1,0:T(8,128)(2,1)S(1)}, s32[16,128]{1,0:T(8,128)S(1)}, f32[32,128]{1,0:T(8,128)S(1)}) custom-call(f32[48,128]{1,0:T(8,128)S(1)} %get-tuple-element.33.refs_0_.own_ref, ...), custom_call_target="tpu_custom_call", output_to_operand_aliasing={{0}: (3, {}), {1}: (4, {}), {2}: (5, {})} | custom-call | flops 4294967296 | bytes 1048576 | tf_op jit(solution)/shard_map/first_near/pallas_call | solution.py:501
  13.1 0.0 collective-permute-done.1.refs_1_.pair
  13.1 4.8 %collective-permute-start.2 = (f32[96,128]{1,0:T(8,128)S(1)}, f32[96,128]{1,0:T(8,128)S(1)}, u32[]{:S(2)}, u32[]{:S(2)}) collective-permute-start(f32[96,128]{1,0:T(8,128)S(1)} %collective-permute-done.1.refs_1_.pair), channel_id=1, source_target_pairs={{0,1},{1,0},{2,3},{3,2},{4,5},{5,4},{6,7},{7,6},{8,9},{9,8},{10,11... | collective-permute-start | bytes 147464 | tf_op jit(solution)/shard_map/ppermute | solution.py:32
  17.9 0.3 first_ahead.1
  18.3 0.5 collective-permute-done.2.forwarded
  18.8 9.5 %first_far.1 = (f32[25,4,64,128]{3,2,1,0:T(8,128)S(1)}, f32[40,8,128]{2,1,0:T(8,128)S(1)}, bf16[40,32,128]{2,1,0:T(8,128)(2,1)S(1)}, s32[16,128]{1,0:T(8,128)S(1...) custom-call(f32[48,128]{1,0:T(8,128)S(1)} %get-tuple-element.33.refs, ...), custom_call_target="tpu_custom_call", output_to_operand_aliasing={{0}: (3, {}), {1}: (7, {}), {2}: (8, {})} | custom-call | flops 4294967296 | bytes 1048576 | tf_op jit(solution)/shard_map/first_far/pallas_call | solution.py:501
  28.3 0.4 collective-permute-start.3
  28.7 0.6 %second_alone.1 = (f32[25,4,64,128]{3,2,1,0:T(8,128)S(1)}, bf16[25,64,32]{2,1,0:T(8,128)(2,1)S(1)}, f32[32,8,128]{2,1,0:T(8,128)S(1)}, bf16[32,32,128]{2,1,0:T(8,128)(2,1)S(1)}) custom-call(f32[36,128]{1,0:T(8,128)S(1)} %get-tuple-element.45.refs_0_.own_ref, f32[32,128]{1,0:T(8,128)S(1)} %get-tuple-element.41.weight_own_ref.refs_1_.refs_7_), custom_call_target="tpu_custom_call" | custom-call | flops 4194304 | bytes 1048576 | tf_op jit(solution)/shard_map/second_alone/pallas_call | solution.py:501
  29.3 0.2 collective-permute-done.3.refs_1_.sibling_ref
  29.6 0.1 collective-permute-start.4
  29.6 7.3 %second_near.1 = (f32[25,4,64,128]{3,2,1,0:T(8,128)S(1)}, f32[32,8,128]{2,1,0:T(8,128)S(1)}, bf16[32,32,128]{2,1,0:T(8,128)(2,1)S(1)}) custom-call(f32[36,128]{1,0:T(8,128)S(1)} %get-tuple-element.45.refs_0_.own_ref, f32[54,128]{1,0:T(8,128)S(1)} %collective-permute-done.3.refs_1_.sibling_ref, ...), custom_call_target="tpu_custom_call", output_to_operand_aliasing={{0}: (3, {}), {1}: (4, {}), {2}: (5, {})} | custom-call | flops 4294967296 | bytes 1048576 | tf_op jit(solution)/shard_map/second_near/pallas_call | solution.py:501
  36.9 0.0 collective-permute-done.4.pair.refs_1_
  36.9 1.0 %collective-permute-start.5 = (f32[90,128]{1,0:T(8,128)S(1)}, f32[90,128]{1,0:T(8,128)S(1)}, u32[]{:S(2)}, u32[]{:S(2)}) collective-permute-start(f32[90,128]{1,0:T(8,128)S(1)} %collective-permute-done.4.pair.refs_1_), channel_id=1, source_target_pairs={{0,1},{1,0},{2,3},{3,2},{4,5},{5,4},{6,7},{7,6},{8,9},{9,8},{10,11... | collective-permute-start | bytes 138248 | tf_op jit(solution)/shard_map/ppermute | solution.py:32
  37.9 0.3 second_ahead.1
  38.3 0.5 collective-permute-done.5.forwarded
  38.8 8.8 %second_far.1 = (f32[25,4,64,128]{3,2,1,0:T(8,128)S(1)}, f32[40,8,128]{2,1,0:T(8,128)S(1)}, bf16[40,32,128]{2,1,0:T(8,128)(2,1)S(1)}, f32[6,12,128]{2,1,0:T(8,12...) custom-call(f32[36,128]{1,0:T(8,128)S(1)} %get-tuple-element.45.refs, ...), custom_call_target="tpu_custom_call", output_to_operand_aliasing={{0}: (3, {}), {1}: (9, {}), {2}: (10, {})} | custom-call | flops 4294967296 | bytes 1048576 | tf_op jit(solution)/shard_map/second_far/pallas_call | solution.py:501
  47.6 0.4 collective-permute-start.6
  48.0 5.7 %collective-permute-start.7 = (f32[36,128]{1,0:T(8,128)S(1)}, f32[36,128]{1,0:T(8,128)S(1)}, u32[]{:S(2)}, u32[]{:S(2)}) collective-permute-start(f32[36,128]{1,0:T(8,128)S(1)} %get-tuple-element.63), channel_id=1, source_target_pairs={{1,2},{2,1},{3,4},{4,3},{5,6},{6,5},{7,8},{8,7},{9,10},{10,9},{11,... | collective-permute-start | bytes 55304 | tf_op jit(solution)/shard_map/ppermute | solution.py:32
  53.7 1.4 %first_place.1 = f32[6,24,128]{2,1,0:T(8,128)} custom-call(s32[2,32]{1,0:T(2,128)} %cuts_ref.3, f32[36,128]{1,0:T(8,128)S(1)} %get-tuple-element.45.refs_0_.own_ref, f32[36,128]{1,0:T(8,128)S(1)} %get-tuple-element.46.speed_ref, f32[54,128]{1,0:T(8,128)S(1)} %collective-permute-done.3.refs_1_.sibling_ref, f32[90,128]{1,0:T(8,128)S(1)} %collective-permute-done.4.pair.refs_1_), custom_call_target="tpu_custom_call" | custom-call | flops 4194304 | bytes 1048576 | tf_op jit(solution)/shard_map/first_place/pallas_call | solution.py:501
  55.0 0.0 collective-permute-done.6.sibling_ref
  55.0 0.1 collective-permute-done.7.beside_ref
  55.1 1.3 %place.1 = f32[6,24,128]{2,1,0:T(8,128)} custom-call(s32[2,32]{1,0:T(2,128)} %cuts_ref.3, f32[36,128]{1,0:T(8,128)S(1)} %collective-permute-done.6.sibling_ref, f32[6,12,128]{2,1,0:T(8,128)S(1)} %get-tuple-element.62.own_ref, f32[36,128]{1,0:T(8,128)S(1)} %collective-permute-done.7.beside_ref), custom_call_target="tpu_custom_call" | custom-call | bytes 1048576 | tf_op jit(solution)/shard_map/place/pallas_call | solution.py:501
  (3 shorter events, 0.0 us)
Async XLA Ops:
  1.5 1.3 %collective-permute-start = (f32[48,128]{1,0:T(8,128)S(1)}, f32[48,128]{1,0:T(8,128)S(1)}, u32[]{:S(2)}, u32[]{:S(2)}) collective-permute-start(f32[48,128]{1,0:T(8,128)S(1)} %get-tuple-element.33.refs_0_.own_ref), channel_id=1, source_target_pairs={{0,1},{1,0},{2,3},{3,2},{4,5},{5,4},{6,7},{7,6},{8,9},{9,8},{10,11... | collective-permute-start | bytes 73736 | tf_op jit(solution)/shard_map/ppermute | solution.py:32
  2.7 10.4 %collective-permute-start.1 = (f32[96,128]{1,0:T(8,128)S(1)}, f32[96,128]{1,0:T(8,128)S(1)}, u32[]{:S(2)}, u32[]{:S(2)}) collective-permute-start(f32[96,128]{1,0:T(8,128)S(1)} %pad_maximum_fusion), channel_id=1, source_target_pairs={{1,2},{2,1},{3,4},{4,3},{5,6},{6,5},{7,8},{8,7},{9,10},{10,9},{11,... | collective-permute-start | bytes 147464 | tf_op jit(solution)/shard_map/ppermute | solution.py:32
  13.1 5.7 %collective-permute-start.2 = (f32[96,128]{1,0:T(8,128)S(1)}, f32[96,128]{1,0:T(8,128)S(1)}, u32[]{:S(2)}, u32[]{:S(2)}) collective-permute-start(f32[96,128]{1,0:T(8,128)S(1)} %collective-permute-done.1.refs_1_.pair), channel_id=1, source_target_pairs={{0,1},{1,0},{2,3},{3,2},{4,5},{5,4},{6,7},{7,6},{8,9},{9,8},{10,11... | collective-permute-start | bytes 147464 | tf_op jit(solution)/shard_map/ppermute | solution.py:32
  28.3 1.3 %collective-permute-start.3 = (f32[54,128]{1,0:T(8,128)S(1)}, f32[54,128]{1,0:T(8,128)S(1)}, u32[]{:S(2)}, u32[]{:S(2)}) collective-permute-start(f32[54,128]{1,0:T(8,128)S(1)} %get-tuple-element.47), channel_id=1, source_target_pairs={{0,1},{1,0},{2,3},{3,2},{4,5},{5,4},{6,7},{7,6},{8,9},{9,8},{10,11... | collective-permute-start | bytes 82952 | tf_op jit(solution)/shard_map/ppermute | solution.py:32
  29.6 7.4 %collective-permute-start.4 = (f32[90,128]{1,0:T(8,128)S(1)}, f32[90,128]{1,0:T(8,128)S(1)}, u32[]{:S(2)}, u32[]{:S(2)}) collective-permute-start(f32[90,128]{1,0:T(8,128)S(1)} %pad_maximum_fusion.1), channel_id=1, source_target_pairs={{1,2},{2,1},{3,4},{4,3},{5,6},{6,5},{7,8},{8,7},{9,10},{10,9},{11,... | collective-permute-start | bytes 138248 | tf_op jit(solution)/shard_map/ppermute | solution.py:32
  36.9 1.9 %collective-permute-start.5 = (f32[90,128]{1,0:T(8,128)S(1)}, f32[90,128]{1,0:T(8,128)S(1)}, u32[]{:S(2)}, u32[]{:S(2)}) collective-permute-start(f32[90,128]{1,0:T(8,128)S(1)} %collective-permute-done.4.pair.refs_1_), channel_id=1, source_target_pairs={{0,1},{1,0},{2,3},{3,2},{4,5},{5,4},{6,7},{7,6},{8,9},{9,8},{10,11... | collective-permute-start | bytes 138248 | tf_op jit(solution)/shard_map/ppermute | solution.py:32
  47.6 7.4 %collective-permute-start.6 = (f32[36,128]{1,0:T(8,128)S(1)}, f32[36,128]{1,0:T(8,128)S(1)}, u32[]{:S(2)}, u32[]{:S(2)}) collective-permute-start(f32[36,128]{1,0:T(8,128)S(1)} %get-tuple-element.61), channel_id=1, source_target_pairs={{0,1},{1,0},{2,3},{3,2},{4,5},{5,4},{6,7},{7,6},{8,9},{9,8},{10,11... | collective-permute-start | bytes 55304 | tf_op jit(solution)/shard_map/ppermute | solution.py:32
  48.0 7.1 %collective-permute-start.7 = (f32[36,128]{1,0:T(8,128)S(1)}, f32[36,128]{1,0:T(8,128)S(1)}, u32[]{:S(2)}, u32[]{:S(2)}) collective-permute-start(f32[36,128]{1,0:T(8,128)S(1)} %get-tuple-element.63), channel_id=1, source_target_pairs={{1,2},{2,1},{3,4},{4,3},{5,6},{6,5},{7,8},{8,7},{9,10},{10,9},{11,... | collective-permute-start | bytes 55304 | tf_op jit(solution)/shard_map/ppermute | solution.py:32

commit v5 on v4

--- a/solution.py
+++ b/solution.py
@@ -14,7 +14,7 @@
 time_step = 0.5
 reach = 2
 chunk = 4
-units = 8
+units = 12
 feature_rows = 32
 far_norm = 1e36
 lanes = 128

time: 57.2 us -> 54.3 us (0.949)
  starting transfers between devices: 15.1 us -> 11.2 us
  Pallas kernels: 38.8 us -> 39.5 us
    ppermute x8, starting transfers between devices: 15.1 us -> 11.2 us  [swapped(): return lax.ppermute(value, AXES, pairs)]
    pallas_call x10, Pallas kernels: 37.9 us -> 38.6 us  [call(): pl.pallas_call(kernel, out_shape=outs, in_specs=[kind for kind, _ in ins]...]
  transfers between devices with their start and end apart: 8 -> 8, of which waited for: 5 -> 5; matrix products, arithmetic and copies ran while one was open for 0% -> 0% of each run, Pallas kernels for 32% -> 35%
where the time goes in v5:
time: 54.3 us; the launch traced here: 53.8 us
  Pallas kernels  39.5 us (73%)
  starting transfers between devices  11.2 us (21%)
  waiting for transfers between devices  2.4 us (4%)
  between operations  0.76 us (1%)
    pallas_call x10, Pallas kernels, call(): pl.pallas_call(kernel, out_shape=outs, in_specs=[kind for kind, _ in ins]...  38.6 us
    ppermute x8, starting transfers between devices, swapped(): return lax.ppermute(value, AXES, pairs)  11.2 us
    ppermute x8, waiting for transfers between devices, swapped(): return lax.ppermute(value, AXES, pairs)  2.4 us
  transfers between devices with their start and end apart: 8, of which 5 were waited for; matrix products, arithmetic and copies ran while one was open for 0% of the time, Pallas kernels for 35%

profile of v5, /device:TPU:1, one launch (start us, length us, event | category | flops | bytes accessed | tf_op | source)
XLA Modules:
  0.0 53.8 jit_solution(4374404285655362252)
XLA Ops:
  0.6 0.8 %pack.1 = (f32[48,128]{1,0:T(8,128)S(1)}, f32[36,128]{1,0:T(8,128)S(1)}) custom-call(f32[12,6,128]{2,1,0:T(8,128)} %particles_ref.1, s32[12]{0:T(128)} %occupancy_ref.1, s32[12,16]{1,0:T(8,128)} %neighbours_ref.1), custom_call_target="tpu_custom_call" | custom-call | tf_op jit(solution)/shard_map/pack/pallas_call | solution.py:530
  1.5 0.1 collective-permute-start
  1.6 0.6 %first_alone.1 = (f32[25,4,64,128]{3,2,1,0:T(8,128)S(1)}, bf16[25,64,32]{2,1,0:T(8,128)(2,1)S(1)}, f32[32,8,128]{2,1,0:T(8,128)S(1)}, bf16[32,32,128]{2,1,0:T(8,128)(2,1)S(1)}) custom-call(f32[48,128]{1,0:T(8,128)S(1)} %get-tuple-element.33.refs_0_.own_ref), custom_call_target="tpu_custom_call" | custom-call | flops 4194304 | bytes 1048576 | tf_op jit(solution)/shard_map/first_alone/pallas_call | solution.py:501
  2.3 0.5 collective-permute-done.refs_1_
  2.7 2.6 %collective-permute-start.1 = (f32[96,128]{1,0:T(8,128)S(1)}, f32[96,128]{1,0:T(8,128)S(1)}, u32[]{:S(2)}, u32[]{:S(2)}) collective-permute-start(f32[96,128]{1,0:T(8,128)S(1)} %pad_maximum_fusion), channel_id=1, source_target_pairs={{1,2},{2,1},{3,4},{4,3},{5,6},{6,5},{7,8},{8,7},{9,10},{10,9},{11,... | collective-permute-start | bytes 147464 | tf_op jit(solution)/shard_map/ppermute | solution.py:32
  5.3 8.1 %first_near.1 = (f32[25,4,64,128]{3,2,1,0:T(8,128)S(1)}, f32[32,8,128]{2,1,0:T(8,128)S(1)}, bf16[32,32,128]{2,1,0:T(8,128)(2,1)S(1)}, s32[16,128]{1,0:T(8,128)S(1)}, f32[32,128]{1,0:T(8,128)S(1)}) custom-call(f32[48,128]{1,0:T(8,128)S(1)} %get-tuple-element.33.refs_0_.own_ref, ...), custom_call_target="tpu_custom_call", output_to_operand_aliasing={{0}: (3, {}), {1}: (4, {}), {2}: (5, {})} | custom-call | flops 4294967296 | bytes 1048576 | tf_op jit(solution)/shard_map/first_near/pallas_call | solution.py:501
  13.4 0.0 collective-permute-done.1.refs_1_.pair
  13.4 4.2 %collective-permute-start.2 = (f32[96,128]{1,0:T(8,128)S(1)}, f32[96,128]{1,0:T(8,128)S(1)}, u32[]{:S(2)}, u32[]{:S(2)}) collective-permute-start(f32[96,128]{1,0:T(8,128)S(1)} %collective-permute-done.1.refs_1_.pair), channel_id=1, source_target_pairs={{0,1},{1,0},{2,3},{3,2},{4,5},{5,4},{6,7},{7,6},{8,9},{9,8},{10,11... | collective-permute-start | bytes 147464 | tf_op jit(solution)/shard_map/ppermute | solution.py:32
  17.7 0.3 first_ahead.1
  18.0 0.5 collective-permute-done.2.forwarded
  18.5 9.6 %first_far.1 = (f32[25,4,64,128]{3,2,1,0:T(8,128)S(1)}, f32[40,8,128]{2,1,0:T(8,128)S(1)}, bf16[40,32,128]{2,1,0:T(8,128)(2,1)S(1)}, s32[16,128]{1,0:T(8,128)S(1...) custom-call(f32[48,128]{1,0:T(8,128)S(1)} %get-tuple-element.33.refs, ...), custom_call_target="tpu_custom_call", output_to_operand_aliasing={{0}: (3, {}), {1}: (7, {}), {2}: (8, {})} | custom-call | flops 4294967296 | bytes 1048576 | tf_op jit(solution)/shard_map/first_far/pallas_call | solution.py:501
  28.2 0.1 collective-permute-start.3
  28.3 0.6 %second_alone.1 = (f32[25,4,64,128]{3,2,1,0:T(8,128)S(1)}, bf16[25,64,32]{2,1,0:T(8,128)(2,1)S(1)}, f32[32,8,128]{2,1,0:T(8,128)S(1)}, bf16[32,32,128]{2,1,0:T(8,128)(2,1)S(1)}) custom-call(f32[36,128]{1,0:T(8,128)S(1)} %get-tuple-element.45.refs_0_.own_ref, f32[32,128]{1,0:T(8,128)S(1)} %get-tuple-element.41.weight_own_ref.refs_1_.refs_7_), custom_call_target="tpu_custom_call" | custom-call | flops 4194304 | bytes 1048576 | tf_op jit(solution)/shard_map/second_alone/pallas_call | solution.py:501
  28.9 0.5 %collective-permute-done.3.refs_1_.sibling_ref = f32[54,128]{1,0:T(8,128)S(1)} collective-permute-done((f32[54,128]{1,0:T(8,128)S(1)}, f32[54,128]{1,0:T(8,128)S(1)}, u32[]{:S(2)}, u32[]{:S(2)}) %collective-permute-start.3) | collective-permute-done | bytes 27680 | tf_op jit(solution)/shard_map/ppermute | solution.py:32
  29.5 0.1 collective-permute-start.4
  29.5 7.3 %second_near.1 = (f32[25,4,64,128]{3,2,1,0:T(8,128)S(1)}, f32[32,8,128]{2,1,0:T(8,128)S(1)}, bf16[32,32,128]{2,1,0:T(8,128)(2,1)S(1)}) custom-call(f32[36,128]{1,0:T(8,128)S(1)} %get-tuple-element.45.refs_0_.own_ref, f32[54,128]{1,0:T(8,128)S(1)} %collective-permute-done.3.refs_1_.sibling_ref, ...), custom_call_target="tpu_custom_call", output_to_operand_aliasing={{0}: (3, {}), {1}: (4, {}), {2}: (5, {})} | custom-call | flops 4294967296 | bytes 1048576 | tf_op jit(solution)/shard_map/second_near/pallas_call | solution.py:501
  36.8 0.0 collective-permute-done.4.pair.refs_1_
  36.8 0.2 collective-permute-start.5
  37.0 0.3 second_ahead.1
  37.4 0.7 %collective-permute-done.5.forwarded = f32[90,128]{1,0:T(8,128)S(1)} collective-permute-done((f32[90,128]{1,0:T(8,128)S(1)}, f32[90,128]{1,0:T(8,128)S(1)}, u32[]{:S(2)}, u32[]{:S(2)}) %collective-permute-start.5) | collective-permute-done | bytes 46112 | tf_op jit(solution)/shard_map/ppermute | solution.py:32
  38.1 9.0 %second_far.1 = (f32[25,4,64,128]{3,2,1,0:T(8,128)S(1)}, f32[40,8,128]{2,1,0:T(8,128)S(1)}, bf16[40,32,128]{2,1,0:T(8,128)(2,1)S(1)}, f32[6,12,128]{2,1,0:T(8,12...) custom-call(f32[36,128]{1,0:T(8,128)S(1)} %get-tuple-element.45.refs, ...), custom_call_target="tpu_custom_call", output_to_operand_aliasing={{0}: (3, {}), {1}: (9, {}), {2}: (10, {})} | custom-call | flops 4294967296 | bytes 1048576 | tf_op jit(solution)/shard_map/second_far/pallas_call | solution.py:501
  47.2 0.1 collective-permute-start.6
  47.2 3.8 %collective-permute-start.7 = (f32[36,128]{1,0:T(8,128)S(1)}, f32[36,128]{1,0:T(8,128)S(1)}, u32[]{:S(2)}, u32[]{:S(2)}) collective-permute-start(f32[36,128]{1,0:T(8,128)S(1)} %get-tuple-element.63), channel_id=1, source_target_pairs={{1,2},{2,1},{3,4},{4,3},{5,6},{6,5},{7,8},{8,7},{9,10},{10,9},{11,... | collective-permute-start | bytes 55304 | tf_op jit(solution)/shard_map/ppermute | solution.py:32
  51.0 1.4 %first_place.1 = f32[6,24,128]{2,1,0:T(8,128)} custom-call(s32[2,32]{1,0:T(2,128)} %cuts_ref.3, f32[36,128]{1,0:T(8,128)S(1)} %get-tuple-element.45.refs_0_.own_ref, f32[36,128]{1,0:T(8,128)S(1)} %get-tuple-element.46.speed_ref, f32[54,128]{1,0:T(8,128)S(1)} %collective-permute-done.3.refs_1_.sibling_ref, f32[90,128]{1,0:T(8,128)S(1)} %collective-permute-done.4.pair.refs_1_), custom_call_target="tpu_custom_call" | custom-call | flops 4194304 | bytes 1048576 | tf_op jit(solution)/shard_map/first_place/pallas_call | solution.py:501
  52.4 0.0 collective-permute-done.6.sibling_ref
  52.4 0.1 collective-permute-done.7.beside_ref
  52.5 1.3 %place.1 = f32[6,24,128]{2,1,0:T(8,128)} custom-call(s32[2,32]{1,0:T(2,128)} %cuts_ref.3, f32[36,128]{1,0:T(8,128)S(1)} %collective-permute-done.6.sibling_ref, f32[6,12,128]{2,1,0:T(8,128)S(1)} %get-tuple-element.62.own_ref, f32[36,128]{1,0:T(8,128)S(1)} %collective-permute-done.7.beside_ref), custom_call_target="tpu_custom_call" | custom-call | bytes 1048576 | tf_op jit(solution)/shard_map/place/pallas_call | solution.py:501
  (3 shorter events, 0.0 us)
Async XLA Ops:
  1.5 1.3 %collective-permute-start = (f32[48,128]{1,0:T(8,128)S(1)}, f32[48,128]{1,0:T(8,128)S(1)}, u32[]{:S(2)}, u32[]{:S(2)}) collective-permute-start(f32[48,128]{1,0:T(8,128)S(1)} %get-tuple-element.33.refs_0_.own_ref), channel_id=1, source_target_pairs={{0,1},{1,0},{2,3},{3,2},{4,5},{5,4},{6,7},{7,6},{8,9},{9,8},{10,11... | collective-permute-start | bytes 73736 | tf_op jit(solution)/shard_map/ppermute | solution.py:32
  2.7 10.7 %collective-permute-start.1 = (f32[96,128]{1,0:T(8,128)S(1)}, f32[96,128]{1,0:T(8,128)S(1)}, u32[]{:S(2)}, u32[]{:S(2)}) collective-permute-start(f32[96,128]{1,0:T(8,128)S(1)} %pad_maximum_fusion), channel_id=1, source_target_pairs={{1,2},{2,1},{3,4},{4,3},{5,6},{6,5},{7,8},{8,7},{9,10},{10,9},{11,... | collective-permute-start | bytes 147464 | tf_op jit(solution)/shard_map/ppermute | solution.py:32
  13.4 5.1 %collective-permute-start.2 = (f32[96,128]{1,0:T(8,128)S(1)}, f32[96,128]{1,0:T(8,128)S(1)}, u32[]{:S(2)}, u32[]{:S(2)}) collective-permute-start(f32[96,128]{1,0:T(8,128)S(1)} %collective-permute-done.1.refs_1_.pair), channel_id=1, source_target_pairs={{0,1},{1,0},{2,3},{3,2},{4,5},{5,4},{6,7},{7,6},{8,9},{9,8},{10,11... | collective-permute-start | bytes 147464 | tf_op jit(solution)/shard_map/ppermute | solution.py:32
  28.2 1.3 %collective-permute-start.3 = (f32[54,128]{1,0:T(8,128)S(1)}, f32[54,128]{1,0:T(8,128)S(1)}, u32[]{:S(2)}, u32[]{:S(2)}) collective-permute-start(f32[54,128]{1,0:T(8,128)S(1)} %get-tuple-element.47), channel_id=1, source_target_pairs={{0,1},{1,0},{2,3},{3,2},{4,5},{5,4},{6,7},{7,6},{8,9},{9,8},{10,11... | collective-permute-start | bytes 82952 | tf_op jit(solution)/shard_map/ppermute | solution.py:32
  29.5 7.3 %collective-permute-start.4 = (f32[90,128]{1,0:T(8,128)S(1)}, f32[90,128]{1,0:T(8,128)S(1)}, u32[]{:S(2)}, u32[]{:S(2)}) collective-permute-start(f32[90,128]{1,0:T(8,128)S(1)} %pad_maximum_fusion.1), channel_id=1, source_target_pairs={{1,2},{2,1},{3,4},{4,3},{5,6},{6,5},{7,8},{8,7},{9,10},{10,9},{11,... | collective-permute-start | bytes 138248 | tf_op jit(solution)/shard_map/ppermute | solution.py:32
  36.8 1.3 %collective-permute-start.5 = (f32[90,128]{1,0:T(8,128)S(1)}, f32[90,128]{1,0:T(8,128)S(1)}, u32[]{:S(2)}, u32[]{:S(2)}) collective-permute-start(f32[90,128]{1,0:T(8,128)S(1)} %collective-permute-done.4.pair.refs_1_), channel_id=1, source_target_pairs={{0,1},{1,0},{2,3},{3,2},{4,5},{5,4},{6,7},{7,6},{8,9},{9,8},{10,11... | collective-permute-start | bytes 138248 | tf_op jit(solution)/shard_map/ppermute | solution.py:32
  47.2 5.2 %collective-permute-start.6 = (f32[36,128]{1,0:T(8,128)S(1)}, f32[36,128]{1,0:T(8,128)S(1)}, u32[]{:S(2)}, u32[]{:S(2)}) collective-permute-start(f32[36,128]{1,0:T(8,128)S(1)} %get-tuple-element.61), channel_id=1, source_target_pairs={{0,1},{1,0},{2,3},{3,2},{4,5},{5,4},{6,7},{7,6},{8,9},{9,8},{10,11... | collective-permute-start | bytes 55304 | tf_op jit(solution)/shard_map/ppermute | solution.py:32
  47.2 5.2 %collective-permute-start.7 = (f32[36,128]{1,0:T(8,128)S(1)}, f32[36,128]{1,0:T(8,128)S(1)}, u32[]{:S(2)}, u32[]{:S(2)}) collective-permute-start(f32[36,128]{1,0:T(8,128)S(1)} %get-tuple-element.63), channel_id=1, source_target_pairs={{1,2},{2,1},{3,4},{4,3},{5,6},{6,5},{7,8},{8,7},{9,10},{10,9},{11,... | collective-permute-start | bytes 55304 | tf_op jit(solution)/shard_map/ppermute | solution.py:32

commit v6 on v5

--- a/solution.py
+++ b/solution.py
@@ -212,10 +212,10 @@
             for row in range(4):
                 total_ref[spot, row, strip, :] = sums[row]
 
-    def step(_, carry):
+    def step(count, _, carry):
         tile, block, part = carry
         waiting = None
-        for _ in range(units):
+        for _ in range(count):
             sources = sources_of(tile, part)
             places = [
                 [jnp.broadcast_to(moment_ref[source, axis : axis + 1, :], (8, lanes)) for axis in range(3)]
@@ -231,7 +231,10 @@
         return (tile, block, part)
 
     zero = jnp.int32(0)
-    lax.fori_loop(0, (item_total + units - 1) // units, step, (zero, zero, zero))
+    whole = item_total // units
+    few = units // 2
+    carry = lax.fori_loop(0, whole, functools.partial(step, units), (zero, zero, zero))
+    lax.fori_loop(0, (item_total - whole * units + few - 1) // few, functools.partial(step, few), carry)
 
 
 def advance(middle, place_own, speed_own, weight_own, total_ref, sums_ref):

time: 54.3 us -> 53.5 us (0.985); the launches traced: 53.8 us -> 54.1 us
  starting transfers between devices: 11.2 us -> 8.32 us
  waiting for transfers between devices: 2.4 us -> 4.27 us
  Pallas kernels: 39.5 us -> 40.7 us
    ppermute x8, starting transfers between devices: 11.2 us -> 8.32 us  [swapped(): return lax.ppermute(value, AXES, pairs)]
    ppermute x8, waiting for transfers between devices: 2.4 us -> 4.27 us  [swapped(): return lax.ppermute(value, AXES, pairs)]
    pallas_call x10, Pallas kernels: 38.6 us -> 39.9 us  [call(): pl.pallas_call(kernel, out_shape=outs, in_specs=[kind for kind, _ in ins]...]
  transfers between devices with their start and end apart: 8 -> 8, of which waited for: 5 -> 5; matrix products, arithmetic and copies ran while one was open for 0% -> 0% of each run, Pallas kernels for 35% -> 38%
where the time goes in v6:
time: 53.5 us; the launch traced here: 54.1 us
  Pallas kernels  40.7 us (76%)
  starting transfers between devices  8.32 us (16%)
  waiting for transfers between devices  4.27 us (8%)
  between operations  0.76 us (1%)
    pallas_call x10, Pallas kernels, call(): pl.pallas_call(kernel, out_shape=outs, in_specs=[kind for kind, _ in ins]...  39.9 us
    ppermute x8, starting transfers between devices, swapped(): return lax.ppermute(value, AXES, pairs)  8.32 us
    ppermute x8, waiting for transfers between devices, swapped(): return lax.ppermute(value, AXES, pairs)  4.27 us
  transfers between devices with their start and end apart: 8, of which 5 were waited for; matrix products, arithmetic and copies ran while one was open for 0% of the time, Pallas kernels for 38%

profile of v6, /device:TPU:1, one launch (start us, length us, event | category | flops | bytes accessed | tf_op | source)
XLA Modules:
  0.0 54.1 jit_solution(7188992217555369958)
XLA Ops:
  0.6 0.8 %pack.1 = (f32[48,128]{1,0:T(8,128)S(1)}, f32[36,128]{1,0:T(8,128)S(1)}) custom-call(f32[12,6,128]{2,1,0:T(8,128)} %particles_ref.1, s32[12]{0:T(128)} %occupancy_ref.1, s32[12,16]{1,0:T(8,128)} %neighbours_ref.1), custom_call_target="tpu_custom_call" | custom-call | tf_op jit(solution)/shard_map/pack/pallas_call | solution.py:533
  1.5 0.1 collective-permute-start
  1.6 0.6 %first_alone.1 = (f32[25,4,64,128]{3,2,1,0:T(8,128)S(1)}, bf16[25,64,32]{2,1,0:T(8,128)(2,1)S(1)}, f32[32,8,128]{2,1,0:T(8,128)S(1)}, bf16[32,32,128]{2,1,0:T(8,128)(2,1)S(1)}) custom-call(f32[48,128]{1,0:T(8,128)S(1)} %get-tuple-element.33.refs_0_.own_ref), custom_call_target="tpu_custom_call" | custom-call | flops 4194304 | bytes 1048576 | tf_op jit(solution)/shard_map/first_alone/pallas_call | solution.py:504
  2.3 0.5 collective-permute-done.refs_1_
  2.7 2.6 %collective-permute-start.1 = (f32[96,128]{1,0:T(8,128)S(1)}, f32[96,128]{1,0:T(8,128)S(1)}, u32[]{:S(2)}, u32[]{:S(2)}) collective-permute-start(f32[96,128]{1,0:T(8,128)S(1)} %pad_maximum_fusion), channel_id=1, source_target_pairs={{1,2},{2,1},{3,4},{4,3},{5,6},{6,5},{7,8},{8,7},{9,10},{10,9},{11,... | collective-permute-start | bytes 147464 | tf_op jit(solution)/shard_map/ppermute | solution.py:32
  5.3 9.0 %first_near.1 = (f32[25,4,64,128]{3,2,1,0:T(8,128)S(1)}, f32[32,8,128]{2,1,0:T(8,128)S(1)}, bf16[32,32,128]{2,1,0:T(8,128)(2,1)S(1)}, s32[16,128]{1,0:T(8,128)S(1)}, f32[32,128]{1,0:T(8,128)S(1)}) custom-call(f32[48,128]{1,0:T(8,128)S(1)} %get-tuple-element.33.refs_0_.own_ref, ...), custom_call_target="tpu_custom_call", output_to_operand_aliasing={{0}: (3, {}), {1}: (4, {}), {2}: (5, {})} | custom-call | flops 4294967296 | bytes 1048576 | tf_op jit(solution)/shard_map/first_near/pallas_call | solution.py:504
  14.3 0.0 collective-permute-done.1.refs_1_.pair
  14.3 3.4 %collective-permute-start.2 = (f32[96,128]{1,0:T(8,128)S(1)}, f32[96,128]{1,0:T(8,128)S(1)}, u32[]{:S(2)}, u32[]{:S(2)}) collective-permute-start(f32[96,128]{1,0:T(8,128)S(1)} %collective-permute-done.1.refs_1_.pair), channel_id=1, source_target_pairs={{0,1},{1,0},{2,3},{3,2},{4,5},{5,4},{6,7},{7,6},{8,9},{9,8},{10,11... | collective-permute-start | bytes 147464 | tf_op jit(solution)/shard_map/ppermute | solution.py:32
  17.7 0.3 first_ahead.1
  18.1 0.5 collective-permute-done.2.forwarded
  18.6 9.3 %first_far.1 = (f32[25,4,64,128]{3,2,1,0:T(8,128)S(1)}, f32[40,8,128]{2,1,0:T(8,128)S(1)}, bf16[40,32,128]{2,1,0:T(8,128)(2,1)S(1)}, s32[16,128]{1,0:T(8,128)S(1...) custom-call(f32[48,128]{1,0:T(8,128)S(1)} %get-tuple-element.33.refs, ...), custom_call_target="tpu_custom_call", output_to_operand_aliasing={{0}: (3, {}), {1}: (7, {}), {2}: (8, {})} | custom-call | flops 4294967296 | bytes 1048576 | tf_op jit(solution)/shard_map/first_far/pallas_call | solution.py:504
  27.9 0.1 collective-permute-start.3
  28.0 0.6 %second_alone.1 = (f32[25,4,64,128]{3,2,1,0:T(8,128)S(1)}, bf16[25,64,32]{2,1,0:T(8,128)(2,1)S(1)}, f32[32,8,128]{2,1,0:T(8,128)S(1)}, bf16[32,32,128]{2,1,0:T(8,128)(2,1)S(1)}) custom-call(f32[36,128]{1,0:T(8,128)S(1)} %get-tuple-element.45.refs_0_.own_ref, f32[32,128]{1,0:T(8,128)S(1)} %get-tuple-element.41.weight_own_ref.refs_1_.refs_7_), custom_call_target="tpu_custom_call" | custom-call | flops 4194304 | bytes 1048576 | tf_op jit(solution)/shard_map/second_alone/pallas_call | solution.py:504
  28.7 0.5 %collective-permute-done.3.refs_1_.sibling_ref = f32[54,128]{1,0:T(8,128)S(1)} collective-permute-done((f32[54,128]{1,0:T(8,128)S(1)}, f32[54,128]{1,0:T(8,128)S(1)}, u32[]{:S(2)}, u32[]{:S(2)}) %collective-permute-start.3) | collective-permute-done | bytes 27680 | tf_op jit(solution)/shard_map/ppermute | solution.py:32
  29.2 0.1 collective-permute-start.4
  29.3 8.2 %second_near.1 = (f32[25,4,64,128]{3,2,1,0:T(8,128)S(1)}, f32[32,8,128]{2,1,0:T(8,128)S(1)}, bf16[32,32,128]{2,1,0:T(8,128)(2,1)S(1)}) custom-call(f32[36,128]{1,0:T(8,128)S(1)} %get-tuple-element.45.refs_0_.own_ref, f32[54,128]{1,0:T(8,128)S(1)} %collective-permute-done.3.refs_1_.sibling_ref, ...), custom_call_target="tpu_custom_call", output_to_operand_aliasing={{0}: (3, {}), {1}: (4, {}), {2}: (5, {})} | custom-call | flops 4294967296 | bytes 1048576 | tf_op jit(solution)/shard_map/second_near/pallas_call | solution.py:504
  37.5 0.0 collective-permute-done.4.pair.refs_1_
  37.5 0.1 collective-permute-start.5
  37.6 0.3 second_ahead.1
  38.0 0.9 %collective-permute-done.5.forwarded = f32[90,128]{1,0:T(8,128)S(1)} collective-permute-done((f32[90,128]{1,0:T(8,128)S(1)}, f32[90,128]{1,0:T(8,128)S(1)}, u32[]{:S(2)}, u32[]{:S(2)}) %collective-permute-start.5) | collective-permute-done | bytes 46112 | tf_op jit(solution)/shard_map/ppermute | solution.py:32
  38.8 8.7 %second_far.1 = (f32[25,4,64,128]{3,2,1,0:T(8,128)S(1)}, f32[40,8,128]{2,1,0:T(8,128)S(1)}, bf16[40,32,128]{2,1,0:T(8,128)(2,1)S(1)}, f32[6,12,128]{2,1,0:T(8,12...) custom-call(f32[36,128]{1,0:T(8,128)S(1)} %get-tuple-element.45.refs, ...), custom_call_target="tpu_custom_call", output_to_operand_aliasing={{0}: (3, {}), {1}: (9, {}), {2}: (10, {})} | custom-call | flops 4294967296 | bytes 1048576 | tf_op jit(solution)/shard_map/second_far/pallas_call | solution.py:504
  47.6 0.1 collective-permute-start.6
  47.6 1.9 %collective-permute-start.7 = (f32[36,128]{1,0:T(8,128)S(1)}, f32[36,128]{1,0:T(8,128)S(1)}, u32[]{:S(2)}, u32[]{:S(2)}) collective-permute-start(f32[36,128]{1,0:T(8,128)S(1)} %get-tuple-element.63), channel_id=1, source_target_pairs={{1,2},{2,1},{3,4},{4,3},{5,6},{6,5},{7,8},{8,7},{9,10},{10,9},{11,... | collective-permute-start | bytes 55304 | tf_op jit(solution)/shard_map/ppermute | solution.py:32
  49.6 1.4 %first_place.1 = f32[6,24,128]{2,1,0:T(8,128)} custom-call(s32[2,32]{1,0:T(2,128)} %cuts_ref.3, f32[36,128]{1,0:T(8,128)S(1)} %get-tuple-element.45.refs_0_.own_ref, f32[36,128]{1,0:T(8,128)S(1)} %get-tuple-element.46.speed_ref, f32[54,128]{1,0:T(8,128)S(1)} %collective-permute-done.3.refs_1_.sibling_ref, f32[90,128]{1,0:T(8,128)S(1)} %collective-permute-done.4.pair.refs_1_), custom_call_target="tpu_custom_call" | custom-call | flops 4194304 | bytes 1048576 | tf_op jit(solution)/shard_map/first_place/pallas_call | solution.py:504
  50.9 0.0 collective-permute-done.6.sibling_ref
  50.9 1.8 %collective-permute-done.7.beside_ref = f32[36,128]{1,0:T(8,128)S(1)} collective-permute-done((f32[36,128]{1,0:T(8,128)S(1)}, f32[36,128]{1,0:T(8,128)S(1)}, u32[]{:S(2)}, u32[]{:S(2)}) %collective-permute-start.7) | collective-permute-done | bytes 18464 | tf_op jit(solution)/shard_map/ppermute | solution.py:32
  52.7 1.3 %place.1 = f32[6,24,128]{2,1,0:T(8,128)} custom-call(s32[2,32]{1,0:T(2,128)} %cuts_ref.3, f32[36,128]{1,0:T(8,128)S(1)} %collective-permute-done.6.sibling_ref, f32[6,12,128]{2,1,0:T(8,128)S(1)} %get-tuple-element.62.own_ref, f32[36,128]{1,0:T(8,128)S(1)} %collective-permute-done.7.beside_ref), custom_call_target="tpu_custom_call" | custom-call | bytes 1048576 | tf_op jit(solution)/shard_map/place/pallas_call | solution.py:504
  (3 shorter events, 0.0 us)
Async XLA Ops:
  1.5 1.3 %collective-permute-start = (f32[48,128]{1,0:T(8,128)S(1)}, f32[48,128]{1,0:T(8,128)S(1)}, u32[]{:S(2)}, u32[]{:S(2)}) collective-permute-start(f32[48,128]{1,0:T(8,128)S(1)} %get-tuple-element.33.refs_0_.own_ref), channel_id=1, source_target_pairs={{0,1},{1,0},{2,3},{3,2},{4,5},{5,4},{6,7},{7,6},{8,9},{9,8},{10,11... | collective-permute-start | bytes 73736 | tf_op jit(solution)/shard_map/ppermute | solution.py:32
  2.7 11.6 %collective-permute-start.1 = (f32[96,128]{1,0:T(8,128)S(1)}, f32[96,128]{1,0:T(8,128)S(1)}, u32[]{:S(2)}, u32[]{:S(2)}) collective-permute-start(f32[96,128]{1,0:T(8,128)S(1)} %pad_maximum_fusion), channel_id=1, source_target_pairs={{1,2},{2,1},{3,4},{4,3},{5,6},{6,5},{7,8},{8,7},{9,10},{10,9},{11,... | collective-permute-start | bytes 147464 | tf_op jit(solution)/shard_map/ppermute | solution.py:32
  14.3 4.3 %collective-permute-start.2 = (f32[96,128]{1,0:T(8,128)S(1)}, f32[96,128]{1,0:T(8,128)S(1)}, u32[]{:S(2)}, u32[]{:S(2)}) collective-permute-start(f32[96,128]{1,0:T(8,128)S(1)} %collective-permute-done.1.refs_1_.pair), channel_id=1, source_target_pairs={{0,1},{1,0},{2,3},{3,2},{4,5},{5,4},{6,7},{7,6},{8,9},{9,8},{10,11... | collective-permute-start | bytes 147464 | tf_op jit(solution)/shard_map/ppermute | solution.py:32
  27.9 1.3 %collective-permute-start.3 = (f32[54,128]{1,0:T(8,128)S(1)}, f32[54,128]{1,0:T(8,128)S(1)}, u32[]{:S(2)}, u32[]{:S(2)}) collective-permute-start(f32[54,128]{1,0:T(8,128)S(1)} %get-tuple-element.47), channel_id=1, source_target_pairs={{0,1},{1,0},{2,3},{3,2},{4,5},{5,4},{6,7},{7,6},{8,9},{9,8},{10,11... | collective-permute-start | bytes 82952 | tf_op jit(solution)/shard_map/ppermute | solution.py:32
  29.2 8.3 %collective-permute-start.4 = (f32[90,128]{1,0:T(8,128)S(1)}, f32[90,128]{1,0:T(8,128)S(1)}, u32[]{:S(2)}, u32[]{:S(2)}) collective-permute-start(f32[90,128]{1,0:T(8,128)S(1)} %pad_maximum_fusion.1), channel_id=1, source_target_pairs={{1,2},{2,1},{3,4},{4,3},{5,6},{6,5},{7,8},{8,7},{9,10},{10,9},{11,... | collective-permute-start | bytes 138248 | tf_op jit(solution)/shard_map/ppermute | solution.py:32
  37.5 1.3 %collective-permute-start.5 = (f32[90,128]{1,0:T(8,128)S(1)}, f32[90,128]{1,0:T(8,128)S(1)}, u32[]{:S(2)}, u32[]{:S(2)}) collective-permute-start(f32[90,128]{1,0:T(8,128)S(1)} %collective-permute-done.4.pair.refs_1_), channel_id=1, source_target_pairs={{0,1},{1,0},{2,3},{3,2},{4,5},{5,4},{6,7},{7,6},{8,9},{9,8},{10,11... | collective-permute-start | bytes 138248 | tf_op jit(solution)/shard_map/ppermute | solution.py:32
  47.6 3.4 %collective-permute-start.6 = (f32[36,128]{1,0:T(8,128)S(1)}, f32[36,128]{1,0:T(8,128)S(1)}, u32[]{:S(2)}, u32[]{:S(2)}) collective-permute-start(f32[36,128]{1,0:T(8,128)S(1)} %get-tuple-element.61), channel_id=1, source_target_pairs={{0,1},{1,0},{2,3},{3,2},{4,5},{5,4},{6,7},{7,6},{8,9},{9,8},{10,11... | collective-permute-start | bytes 55304 | tf_op jit(solution)/shard_map/ppermute | solution.py:32
  47.6 5.1 %collective-permute-start.7 = (f32[36,128]{1,0:T(8,128)S(1)}, f32[36,128]{1,0:T(8,128)S(1)}, u32[]{:S(2)}, u32[]{:S(2)}) collective-permute-start(f32[36,128]{1,0:T(8,128)S(1)} %get-tuple-element.63), channel_id=1, source_target_pairs={{1,2},{2,1},{3,4},{4,3},{5,6},{6,5},{7,8},{8,7},{9,10},{10,9},{11,... | collective-permute-start | bytes 55304 | tf_op jit(solution)/shard_map/ppermute | solution.py:32
